TPU v7x, 512 devices: a whole 4x8x8 slice. The times are simulated.
512 devices in a mesh: seq: 16 (over x, y_hi, core), vocab: 32 (over y_lo, z).
Axes of the slice: x: 4, y: 8 (y_hi: 2, y_lo: 4; y = y_hi * 4 + y_lo), z: 8, core: 2. Of those that a mesh axis runs over, the one named last changes fastest.
Arguments:
- hidden_states: bfloat16 [384, 2304], P('seq', 'vocab'), may hold values from -6 to 6
- loss_mask: int32 [384], P('seq'), may hold values from 0 to 1, as said below
- teacher_probs: bfloat16 [384, 262144], P('seq', 'vocab'), may hold values from 1.899898e-07 to 1.9073486e-05
- head_weight: bfloat16 [2304, 32, 16, 512], P(None, 'vocab', 'seq'), may hold values from -0.5 to 0.5
Outputs:
- grad_hidden: bfloat16 [384, 2304], P('seq', 'vocab')
- grad_head: bfloat16 [2304, 32, 16, 512], P(None, 'vocab', 'seq')
Inputs may be any that keep to these rules, and one draw needn't show every extreme that they name: `loss_mask`: the last token of the group always counts.
All inputs are finite; a program needn't handle non-finite values.
Results may differ from a plain program's by a relative error of at most 0.0049.
Values may be sent and summed in bfloat16 or wider, within the bound.
No kernel may reach another device: no remote copies, remote signals or barrier semaphores. Data moves between devices by JAX's collectives and lax.ppermute only.
A program may use at most 64 MiB of HBM per device.

v0:
```python
import jax
import jax.numpy as jnp
from jax import lax
from jax.sharding import PartitionSpec as P


def shards(hidden_states, loss_mask, teacher_probs, head_weight):
    seq_count = lax.axis_size("seq")
    vocab_count = lax.axis_size("vocab")
    mask_rows = loss_mask.astype(jnp.bfloat16)
    wide_rows = lax.all_gather(hidden_states, "vocab", axis=1, tiled=True)
    states, mask_all = (
        lax.all_gather(wide_rows, "seq", axis=0, tiled=True),
        lax.all_gather(mask_rows, "seq", axis=0, tiled=True),
    )
    teacher_rows = lax.all_to_all(teacher_probs, "seq", split_axis=1, concat_axis=0, tiled=True)
    feature_dim = head_weight.shape[0]
    shard_cols = head_weight.shape[3]
    weight = head_weight.reshape(feature_dim, shard_cols)
    raw_logits = jnp.dot(states, weight, preferred_element_type=jnp.float32)
    capped_tanh = jnp.tanh(raw_logits / 30.0)
    exp_logits = jnp.exp(30.0 * capped_tanh)
    target = teacher_rows.astype(jnp.float32)
    sum_exp, mass = lax.psum(
        (jnp.sum(exp_logits, axis=1), jnp.sum(target, axis=1)), ("seq", "vocab")
    )
    weights_row = mask_all.astype(jnp.float32)
    masked_count = jnp.sum(weights_row)
    factor = 8.0 * (shard_cols * seq_count * vocab_count) / masked_count
    grad_logits = (
        factor
        * weights_row[:, None]
        * (exp_logits / sum_exp[:, None] * mass[:, None] - target)
        * (1.0 - capped_tanh * capped_tanh)
    ).astype(jnp.bfloat16)
    head_grad = lax.dot_general(
        states, grad_logits, (((0,), (0,)), ((), ())), preferred_element_type=jnp.float32
    )
    grad_head = head_grad.astype(jnp.bfloat16).reshape(head_weight.shape)
    partial_sum = lax.dot_general(
        grad_logits, weight, (((1,), (1,)), ((), ())), preferred_element_type=jnp.float32
    )
    feature_part = lax.psum_scatter(partial_sum, "vocab", scatter_dimension=1, tiled=True)
    grad_hidden = lax.psum_scatter(feature_part, "seq", scatter_dimension=0, tiled=True)
    return (grad_hidden.astype(jnp.bfloat16), grad_head)


def solution(mesh):
    placed = (P("seq", "vocab"), P("seq"), P("seq", "vocab"), P(None, "vocab", "seq", None))
    return jax.shard_map(
        shards,
        mesh=mesh,
        in_specs=placed,
        out_specs=(P("seq", "vocab"), P(None, "vocab", "seq", None)),
        check_vma=False,
    )
```

profile of v0, /device:TPU:64, one launch (start us, length us, event | category | flops | bytes accessed | tf_op | source)
XLA Modules:
  0.0 510.9 jit_solution(17611256485391193726)
XLA Ops:
  7.2 0.0 copy-start
  7.2 0.0 copy-start.1
  7.2 0.0 copy-start.2
  7.2 0.0 all-gather.3.cloned.1.call-start
  7.2 80.5 %all-gather = bf16[32,72,24]{1,2,0:T(8,128)(2,1)S(1)} all-gather(bf16[1,72,24]{1,2,0:T(8,128)(2,1)} %bitcast.48), channel_id=1, replica_groups=mesh['seq'=16,'vocab'=32] {'vocab'}, dimensions={0}, use_global_device_ids=true | all-gather | bytes 114048 | tf_op jit(solution)/shard_map/all_gather | solution.py:11
  87.7 0.9 reshape.27
  88.7 0.0 all-gather.3.cloned.1.call-update
  88.7 1.8 copy.21
  90.4 7.0 %all-to-all-start = ((bf16[24,16,512]{2,0,1:T(8,128)(2,1)}), bf16[24,16,512]{2,0,1:T(8,128)(2,1)S(1)}, u32[]{:S(2)}, u32[]{:S(2)}) async-start(bf16[24,16,512]{2,0,1:T(8,128)(2,1)} %bitcast.44), calls=%async_computation | async-start | bytes 786432 | tf_op jit(solution)/shard_map/all_to_all | solution.py:16
  97.4 0.0 reduce-scatter.6.cloned.1.call-start
  97.5 0.0 copy-done.2
  97.5 0.0 copy-done.1
  97.5 0.7 fusion.15
  98.9 0.2 dynamic-update-slice
  99.2 50.8 %all-reduce = bf16[384]{0:T(512)(128)(2,1)S(1)} all-reduce(bf16[384]{0:T(512)(128)(2,1)S(1)} %dynamic-update-slice), channel_id=1, replica_groups=mesh['seq'=16,'vocab'=32] {'seq'}, use_global_device_ids=true, to_apply=%add | all-reduce | flops 384 | bytes 1536
  150.0 0.7 convert_reduce_fusion.1
  151.4 0.0 all-to-all-done
  151.4 0.1 convert_reduce_fusion
  151.6 0.1 reduce_sum.35
  151.7 0.2 all-gather.3.cloned.1.call-done
  151.9 0.0 copy-done
  151.9 3.5 fusion.14
  155.4 99.5 %all-reduce.3 = (f32[384]{0:T(512)S(1)}, f32[384]{0:T(512)S(1)}) all-reduce(f32[384]{0:T(512)S(1)} %reduce_sum.35, f32[384]{0:T(512)S(1)} %get-tuple-element.12), channel_id=1, replica_groups=mesh['seq'=16,'vocab'=32] {'seq','vocab'}, use_global_device_ids=true, to_apply=%region_4.0 | all-reduce | flops 768 | bytes 6144 | tf_op jit(solution)/shard_map/psum | solution.py:24
  254.9 1.5 fusion.13
  256.5 3.2 fusion.1
  259.7 0.0 reduce-scatter.6.cloned.1.call-update
  260.3 4.3 fusion
  264.7 4.3 copy.16
  268.9 148.8 %reduce-scatter.6.cloned.1.call-done = f32[384,72]{0,1:T(8,128)} async-done(((f32[384,2304]{0,1:T(8,128)}), f32[384,72]{0,1:T(8,128)}) %reduce-scatter.6.cloned.1.call-update) | async-done | bytes 110608
  417.7 85.6 %all-reduce.2 = bf16[384,72]{0,1:T(8,128)(2,1)S(1)} all-reduce(f32[384,72]{0,1:T(8,128)} %reduce-scatter.6.cloned.1.call-done), channel_id=3, replica_groups=mesh['seq'=16,'vocab'=32] {'seq'}, use_global_device_ids=true, to_apply=%region_6.0.clone | all-reduce | flops 27648 | bytes 165888
  503.3 0.1 dynamic-slice_convert_fusion
  503.4 0.7 copy.15
  (4 shorter events, 0.0 us)
Async XLA Ops:
  7.2 144.7 %copy-start = (bf16[2304,1,1,512]{3,0,2,1:T(8,128)(2,1)S(1)}, bf16[2304,1,1,512]{3,0,2,1:T(8,128)(2,1)}, u32[]{:S(2)}) copy-start(bf16[2304,1,1,512]{3,0,2,1:T(8,128)(2,1)} %param.7) | copy-start | bytes 7077892
  7.2 90.3 %copy-start.1 = (u32[512]{0:T(512)S(1)}, u32[512]{0:T(512)}, u32[]{:S(2)}) copy-start(u32[512]{0:T(512)} %constant.16) | copy-start | bytes 6148
  7.2 90.3 %copy-start.2 = (s32[24]{0:T(128)S(1)}, s32[24]{0:T(128)}, u32[]{:S(2)}) copy-start(s32[24]{0:T(128)} %param.5) | copy-start | bytes 292
  7.2 144.7 %all-gather.3.cloned.1.call-start = ((), (), s32[]{:S(2)}) async-start(), calls=%async_computation.2 | async-start | bytes 1880064 | tf_op jit(solution)/shard_map/all_gather | solution.py:13
  90.4 61.0 %all-to-all-start = ((bf16[24,16,512]{2,0,1:T(8,128)(2,1)}), bf16[24,16,512]{2,0,1:T(8,128)(2,1)S(1)}, u32[]{:S(2)}, u32[]{:S(2)}) async-start(bf16[24,16,512]{2,0,1:T(8,128)(2,1)} %bitcast.44), calls=%async_computation | async-start | bytes 786432 | tf_op jit(solution)/shard_map/all_to_all | solution.py:16
  97.4 320.3 %reduce-scatter.6.cloned.1.call-start = ((), (), s32[]{:S(2)}) async-start(), calls=%async_computation.3 | async-start | bytes 3649536
Sparse Core Ops, SparseCore 0:
  88.8 63.0 all-gather.2
  259.8 157.8 reduce-scatter.5
where the time goes:
time: 511 us
  blocking collectives  316 us (62%)
  waiting for transfers between devices  149 us (29%)
  between operations  16.3 us (3%)
  matrix products  11 us (2%)
  local copies, waits for them, and re-layouts  8.77 us (2%)
  starting transfers between devices  7.05 us (1%)
    unnamed x3, waiting for transfers between devices  149 us
    unnamed x2, blocking collectives  136 us
    psum x1, blocking collectives, shards(): lax.psum((jnp.sum(exp_logits, axis=1), jnp.sum(target, axis=1)), ('seq',...  99.5 us
    all_gather x1, blocking collectives, shards(): wide_rows = lax.all_gather(hidden_states, 'vocab', axis=1, tiled=True)  80.5 us
  transfers between devices with their start and end apart: 3, of which 2 were waited for; matrix products, arithmetic and copies ran while one was open for 2% of the time, Pallas kernels for 0%

commit v1 on v0

v1 whole, which is shorter than its diff:
```python
import jax
import jax.numpy as jnp
from jax import lax
from jax.experimental import pallas as pl
from jax.sharding import Mesh
from jax.sharding import PartitionSpec as P

SIZES = {"x": 4, "yh": 2, "c": 2, "yl": 4, "z": 8}
SEQ = ("x", "yh", "c")
VOCAB = ("yl", "z")
PLANE = ("yh", "yl", "z")
SWAP = [(0, 1), (1, 0)]
f32, bf16 = jnp.float32, jnp.bfloat16


def to_all(block, axes):
    count = 1
    for axis in axes:
        count *= SIZES[axis]
    return lax.all_to_all(
        jnp.broadcast_to(block[None], (count,) + block.shape), axes, 0, 0, tiled=True
    )


def softcap(rows, weight):
    capped_tanh = jnp.tanh(jnp.dot(rows, weight, preferred_element_type=f32) / 30.0)
    return capped_tanh, jnp.exp(30.0 * capped_tanh), 1.0 - capped_tanh * capped_tanh


def terms(exp_logits, target, slope, weight):
    both = jnp.concatenate([exp_logits * slope, target * slope])
    high = both.astype(bf16)
    low = (both - high.astype(f32)).astype(bf16)
    dims = (((1,), (1,)), ((), ()))
    return lax.dot_general(high, weight, dims, preferred_element_type=f32) + lax.dot_general(
        low, weight, dims, preferred_element_type=f32
    )


def packed(block):
    first, second, third = block[:8], block[8:16], block[16:]
    top = jnp.concatenate([first, second[:, :56]], axis=1)
    rest = jnp.concatenate([second[:, 56:], third, jnp.zeros((8, 40), block.dtype)], axis=1)
    return jnp.concatenate([top, rest], axis=0)


def unpacked(block):
    top, rest = block[..., :8, :], block[..., 8:, :]
    second = jnp.concatenate([top[..., 72:], rest[..., :16]], axis=-1)
    return jnp.concatenate([top[..., :72], second, rest[..., 16:88]], axis=-2)


def pack_copies_kernel(block_ref, out_ref):
    block = packed(block_ref[...].astype(f32)).astype(bf16)
    out_ref[...] = jnp.broadcast_to(block[None], out_ref.shape)


def pack_copies(block):
    out = jax.ShapeDtypeStruct((64, 16, 128), bf16)
    return pl.pallas_call(pack_copies_kernel, out_shape=out)(block)


def sum_pack_kernel(parts_ref, out_ref):
    for y_at in range(2):
        rows = pl.ds(24 * y_at, 24)
        total = parts_ref[0, rows, :].astype(f32)
        for x_at in range(1, 4):
            total = total + parts_ref[x_at, rows, :].astype(f32)
        for shard in range(32):
            out_ref[32 * y_at + shard] = packed(total[:, 72 * shard : 72 * shard + 72]).astype(bf16)


def sum_pack(parts):
    out = jax.ShapeDtypeStruct((64, 16, 128), bf16)
    return pl.pallas_call(sum_pack_kernel, out_shape=out)(parts)


def sum_unpack_kernel(parts_ref, out_ref):
    total = parts_ref[0].astype(f32)
    for at in range(1, 64):
        total = total + parts_ref[at].astype(f32)
    out_ref[...] = unpacked(total).astype(bf16)


def sum_unpack(parts):
    out = jax.ShapeDtypeStruct((24, 72), bf16)
    return pl.pallas_call(sum_unpack_kernel, out_shape=out)(parts)


def shards(hidden_states, loss_mask, teacher_probs, head_weight):
    tokens, features = hidden_states.shape
    feature_dim, shard_cols = head_weight.shape[0], head_weight.shape[3]
    half = 8 * tokens
    weight = head_weight.reshape(feature_dim, shard_cols)
    y_at, core = lax.axis_index("yh"), lax.axis_index("c")

    plane = unpacked(lax.all_to_all(pack_copies(hidden_states), PLANE, 0, 0, tiled=True))
    plane = plane.reshape(2, 32, tokens, features)
    rows = plane.transpose(0, 2, 1, 3).reshape(2 * tokens, feature_dim)

    by_owner = teacher_probs.reshape(tokens, 4, 2, 2, shard_cols)

    def piece(other_y, other_core):
        start = (0, 0, y_at ^ other_y, core ^ other_core, 0)
        block = lax.dynamic_slice(by_owner, start, (tokens, 4, 1, 1, shard_cols))
        block = block.reshape(tokens, 4, shard_cols).transpose(1, 0, 2)
        if not (other_y or other_core):
            return block
        step = 2 * other_y + other_core
        return lax.ppermute(block, ("yh", "c"), [(i, i ^ step) for i in range(4)])

    def both_y(other_core):
        near, far = piece(0, other_core), piece(1, other_core)
        low, high = jnp.where(y_at == 0, near, far), jnp.where(y_at == 0, far, near)
        return jnp.concatenate([low, high], axis=1)

    mass_part = jnp.sum(teacher_probs.astype(f32), axis=1)

    sent = jnp.concatenate(
        [jnp.broadcast_to(rows[None], (4,) + rows.shape), both_y(0), both_y(1)], axis=2
    )
    got = lax.all_to_all(sent, "x", 0, 0, tiled=True).reshape(half, feature_dim + 2 * shard_cols)
    mine = got[:, :feature_dim]
    other = lax.ppermute(mine, "c", SWAP)
    target_mine = got[:, feature_dim : feature_dim + shard_cols].astype(f32)
    target_other = got[:, feature_dim + shard_cols :].astype(f32)

    tanh_mine, exp_mine, slope_mine = softcap(mine, weight)
    tanh_other, exp_other, slope_other = softcap(other, weight)

    stats = jnp.concatenate(
        [
            jnp.sum(exp_mine, axis=1),
            jnp.sum(exp_other, axis=1),
            mass_part,
            jnp.zeros((128 - tokens,), f32),
        ]
    ).reshape(4, 128)
    stats = jnp.sum(to_all(stats, VOCAB), axis=0)
    masks = jnp.concatenate(
        [jnp.zeros((tokens,), f32), loss_mask.astype(f32), jnp.zeros((128 - 2 * tokens,), f32)]
    )
    stats = jnp.concatenate([stats[:3], stats[3:] + masks[None]])
    stats, terms_mine, terms_other = lax.optimization_barrier(
        (
            stats,
            terms(exp_mine, target_mine, slope_mine, weight),
            terms(exp_other, target_other, slope_other, weight),
        )
    )
    stats = to_all(stats, SEQ)
    sums = jnp.sum(stats[:, :3].reshape(8, 2, 2, half), axis=0)
    sum_mine = jnp.where(core == 0, sums[0, 0] + sums[1, 1], sums[1, 0] + sums[0, 1])
    sum_other = jnp.where(core == 0, sums[0, 1] + sums[1, 0], sums[1, 1] + sums[0, 0])

    def by_core(values):
        values = values.reshape(8, 2, tokens)
        zero, one = values[:, 0].reshape(half), values[:, 1].reshape(half)
        return jnp.where(core == 0, zero, one), jnp.where(core == 0, one, zero)

    mass_mine, mass_other = by_core(stats[:, 3, :tokens])
    mask_mine, mask_other = by_core(stats[:, 3, tokens : 2 * tokens])
    both = terms_mine + lax.ppermute(terms_other, "c", SWAP)

    masked_count = jnp.sum(mask_mine) + jnp.sum(mask_other)
    factor = 8.0 * (shard_cols * 512) / masked_count

    def logit_grad(sum_exp, mass, mask, exp_logits, target, slope):
        return (
            factor
            * mask[:, None]
            * (exp_logits / sum_exp[:, None] * mass[:, None] - target)
            * slope
        ).astype(bf16)

    grad_logits = jnp.concatenate(
        [
            logit_grad(sum_mine, mass_mine, mask_mine, exp_mine, target_mine, slope_mine),
            logit_grad(sum_other, mass_other, mask_other, exp_other, target_other, slope_other),
        ]
    )
    states = jnp.concatenate([mine, other])
    head_grad = lax.dot_general(
        states, grad_logits, (((0,), (0,)), ((), ())), preferred_element_type=f32
    )
    grad_head = head_grad.astype(bf16).reshape(head_weight.shape)

    ratio = (mass_mine / sum_mine)[:, None]
    part = (factor * mask_mine)[:, None] * (both[:half] * ratio - both[half:])
    part = part.astype(bf16).reshape(4, 2 * tokens, feature_dim)
    part = sum_pack(lax.all_to_all(part, "x", 0, 0, tiled=True))
    grad_hidden = sum_unpack(lax.all_to_all(part, PLANE, 0, 0, tiled=True))
    return grad_hidden, grad_head


def solution(mesh):
    fine = Mesh(mesh.devices.reshape(tuple(SIZES.values())), tuple(SIZES))
    head = P(None, VOCAB, SEQ, None)
    return jax.shard_map(
        shards,
        mesh=fine,
        in_specs=(P(SEQ, VOCAB), P(SEQ), P(SEQ, VOCAB), head),
        out_specs=(P(SEQ, VOCAB), head),
        check_vma=False,
    )
```

time: 511 us -> 162 us (0.32)
  the two profiles are of different devices: /device:TPU:64 before, /device:TPU:2 now
where the time goes in v1:
time: 162 us; the launch traced here: 161 us
  starting transfers between devices  60.5 us (37%)
  blocking collectives  38.1 us (24%)
  waiting for transfers between devices  23.2 us (14%)
  matrix products  15.7 us (10%)
  other arithmetic  8.52 us (5%)
  local copies, waits for them, and re-layouts  7.04 us (4%)
  Pallas kernels  5.26 us (3%)
  between operations  2.36 us (1%)
    all_to_all x1, blocking collectives, shards(): lax.all_to_all(sent, 'x', 0, 0, tiled=True)  20.9 us
    all_to_all x2, starting transfers between devices, to_all(): lax.all_to_all(jnp.broadcast_to(block[None], (count,) + block.shape), axe...  18.2 us
    ppermute x3, starting transfers between devices, piece(): return lax.ppermute(block, ('yh', 'c'), [(i, i ^ step) for i in range(4)])  17.2 us
    all_to_all x1, blocking collectives, shards(): part = sum_pack(lax.all_to_all(part, 'x', 0, 0, tiled=True))  17.1 us
    all_to_all x1, starting transfers between devices, shards(): lax.all_to_all(pack_copies(hidden_states), PLANE, 0, 0, tiled=True)  11.7 us
    all_to_all x2, waiting for transfers between devices, to_all(): lax.all_to_all(jnp.broadcast_to(block[None], (count,) + block.shape), axe...  9.7 us
    all_to_all x1, starting transfers between devices, shards(): grad_hidden = sum_unpack(lax.all_to_all(part, PLANE, 0, 0, tiled=True))  9.62 us
    all_to_all x1, waiting for transfers between devices, shards(): grad_hidden = sum_unpack(lax.all_to_all(part, PLANE, 0, 0, tiled=True))  8.57 us
  transfers between devices with their start and end apart: 9, of which 6 were waited for; matrix products, arithmetic and copies ran while one was open for 12% of the time, Pallas kernels for 1%

profile of v1, /device:TPU:2, one launch (start us, length us, event | category | flops | bytes accessed | tf_op | source)
XLA Modules:
  0.0 160.7 jit_solution(15192195199659556169)
XLA Ops:
  0.7 1.4 reshape.152
  2.1 0.8 constant_dynamic-slice_fusion.3
  2.9 0.7 copy.38
  3.6 7.7 %collective-permute-start = (bf16[4,24,512]{2,1,0:T(8,128)(2,1)}, bf16[4,24,512]{2,1,0:T(8,128)(2,1)S(1)}, u32[]{:S(2)}, u32[]{:S(2)}) collective-permute-start(bf16[4,24,512]{2,1,0:T(8,128)(2,1)} %bitcast.63), channel_id=1, source_target_pairs={{0,64},{32,96},{64,0},{96,32},{1,65},{33,97},{65,1},{97,33},{2,66}... | collective-permute-start | bytes 294920 | tf_op jit(solution)/shard_map/ppermute | solution.py:110
  11.4 1.5 shard_map.59
  12.8 11.7 %all-to-all-start = ((bf16[64,16,128]{2,1,0:T(8,128)(2,1)}), bf16[64,16,128]{2,1,0:T(8,128)(2,1)S(1)}, u32[]{:S(2)}, u32[]{:S(2)}) async-start(bf16[64,16,128]{2,1,0:T(8,128)(2,1)} %shard_map.59), calls=%async_computation | async-start | bytes 524288 | tf_op jit(solution)/shard_map/all_to_all | solution.py:97
  24.5 0.7 copy.37
  25.2 1.9 %collective-permute-start.1 = (bf16[4,24,512]{2,1,0:T(8,128)(2,1)}, bf16[4,24,512]{2,1,0:T(8,128)(2,1)S(1)}, u32[]{:S(2)}, u32[]{:S(2)}) collective-permute-start(bf16[4,24,512]{2,1,0:T(8,128)(2,1)} %bitcast.62), channel_id=1, source_target_pairs={{0,32},{32,0},{64,96},{96,64},{1,33},{33,1},{65,97},{97,65},{2,34}... | collective-permute-start | bytes 294920 | tf_op jit(solution)/shard_map/ppermute | solution.py:110
  27.2 7.6 %collective-permute-start.2 = (bf16[4,24,512]{2,1,0:T(8,128)(2,1)S(1)}, bf16[4,24,512]{2,1,0:T(8,128)(2,1)}, u32[]{:S(2)}, u32[]{:S(2)}) collective-permute-start(bf16[4,24,512]{2,1,0:T(8,128)(2,1)S(1)} %bitcast.74), channel_id=1, source_target_pairs={{0,96},{32,64},{64,32},{96,0},{1,97},{33,65},{65,33},{97,1},{2,98}... | collective-permute-start | bytes 294920 | tf_op jit(solution)/shard_map/ppermute | solution.py:110
  34.9 2.9 %collective-permute-done.2 = bf16[4,24,512]{2,1,0:T(8,128)(2,1)} collective-permute-done((bf16[4,24,512]{2,1,0:T(8,128)(2,1)S(1)}, bf16[4,24,512]{2,1,0:T(8,128)(2,1)}, u32[]{:S(2)}, u32[]{:S(2)}) %collective-permute-start.2) | collective-permute-done | bytes 98336 | tf_op jit(solution)/shard_map/ppermute | solution.py:110
  37.7 0.9 broadcast_select_fusion.1
  38.6 0.6 all-to-all-done
  39.3 0.1 slice.99
  39.4 0.1 fusion.56
  39.5 0.1 pad_maximum_fusion.2
  39.7 0.5 broadcast_in_dim.16
  40.2 0.1 maximum_maximum_fusion
  40.4 20.9 %all_to_all.30 = bf16[4,48,3328]{2,1,0:T(8,128)(2,1)S(1)} all-to-all(bf16[4,48,3328]{2,1,0:T(8,128)(2,1)S(1)} %maximum_maximum_fusion), channel_id=1, replica_groups=mesh['x'=4,'yh'=2,'c'=2,'yl'=4,'z'=8] {'x'}, dimensions={0} | all-to-all | bytes 2555904 | tf_op jit(solution)/shard_map/all_to_all | solution.py:122
  61.4 1.9 %collective-permute-start.3 = (bf16[192,2304]{1,0:T(8,128)(2,1)S(1)}, bf16[192,2304]{1,0:T(8,128)(2,1)S(1)}, u32[]{:S(2)}, u32[]{:S(2)}) collective-permute-start(bf16[192,2304]{1,0:T(8,128)(2,1)S(1)} %slice.102), channel_id=1, source_target_pairs={{0,32},{32,0},{1,33},{33,1},{2,34},{34,2},{3,35},{35,3},{4,36},{36... | collective-permute-start | bytes 2654216 | tf_op jit(solution)/shard_map/ppermute | solution.py:124
  63.3 0.2 convert_reduce_fusion
  63.5 0.6 fusion.19
  64.2 1.5 collective-permute-done.3
  65.7 1.7 %convert_multiply_fusion = (f32[192,512]{1,0:T(8,128)S(1)}, f32[192,512]{1,0:T(8,128)S(1)}, f32[192,512]{1,0:T(8,128)S(1)}, f32[192]{0:T(256)S(1)}, f32[192,512]...) fusion(bf16[192,3328]{1,0:T(8,128)(2,1)S(1)} %bitcast.68, f32[192,512]{1,0:T(8,128)S(1)} %fusion.19, ...), kind=kOutput, calls=%fused_computation.34 | convolution fusion | flops 454459008 | bytes 5998080 | tf_op jit(solution)/shard_map/dot_general | solution.py:26
  67.4 0.6 broadcast_in_dim.20
  68.1 11.2 %all-to-all-start.2 = ((f32[32,4,128]{2,1,0:T(4,128)}), f32[32,4,128]{2,1,0:T(4,128)}, u32[]{:S(2)}, u32[]{:S(2)}) async-start(f32[32,4,128]{2,1,0:T(4,128)} %broadcast_in_dim.20), calls=%async_computation.2 | async-start | bytes 131072 | tf_op jit(solution)/shard_map/all_to_all | solution.py:20
  79.3 2.2 %fusion.2 = f32[384,2304]{1,0:T(8,128)S(1)} fusion(bf16[2304,1,1,512]{3,0,2,1:T(8,128)(2,1)S(1)} %copy-done, f32[192,512]{1,0:T(8,128)S(1)} %get-tuple-element.16, f32[192,512]{1,0:T(8,128)} %get-tuple-element.20), kind=kOutput, calls=%fused_computation.5 | convolution fusion | flops 906756096 | bytes 6684672 | tf_op jit(solution)/shard_map/dot_general | solution.py:35
  81.4 3.0 %convolution_add_fusion = f32[384,2304]{1,0:T(8,128)} fusion(f32[384,2304]{1,0:T(8,128)S(1)} %fusion.2, bf16[2304,1,1,512]{3,0,2,1:T(8,128)(2,1)S(1)} %copy-done, f32[192,512]{1,0:T(8,128)S(1)} %get-tuple-element.16, f32[192,512]{1,0:T(8,128)S(1)} %copy-done.2), kind=kOutput, calls=%fused_computation | convolution fusion | flops 907837440 | bytes 10223616 | tf_op jit(solution)/shard_map/dot_general | solution.py:35
  84.4 1.1 fusion.5
  85.6 2.9 %convolution_add_fusion.1 = f32[384,2304]{1,0:T(8,128)} fusion(f32[384,2304]{1,0:T(8,128)S(1)} %fusion.5, bf16[2304,1,1,512]{3,0,2,1:T(8,128)(2,1)S(1)} %copy-done, f32[192,512]{1,0:T(8,128)S(1)} %get-tuple-element.17, f32[192,512]{1,0:T(8,128)S(1)} %get-tuple-element.18), kind=kOutput, calls=%fused_computation.1 | convolution fusion | flops 907837440 | bytes 10223616 | tf_op jit(solution)/shard_map/dot_general | solution.py:35
  88.5 1.1 all-to-all-done.2
  89.5 0.9 reduce_sum.66
  90.5 1.9 %collective-permute-start.4 = (f32[384,2304]{1,0:T(8,128)}, f32[384,2304]{1,0:T(8,128)}, u32[]{:S(2)}, u32[]{:S(2)}) collective-permute-start(f32[384,2304]{1,0:T(8,128)} %convolution_add_fusion), channel_id=1, source_target_pairs={{0,32},{32,0},{1,33},{33,1},{2,34},{34,2},{3,35},{35,3},{4,36},{36... | collective-permute-start | bytes 10616840 | tf_op jit(solution)/shard_map/ppermute | solution.py:163
  92.4 0.6 broadcast_in_dim.44
  93.0 7.0 %all-to-all-start.3 = ((f32[16,4,128]{2,1,0:T(4,128)}), f32[16,4,128]{2,1,0:T(4,128)S(1)}, u32[]{:S(2)}, u32[]{:S(2)}) async-start(f32[16,4,128]{2,1,0:T(4,128)} %broadcast_in_dim.44), calls=%async_computation.3 | async-start | bytes 65536 | tf_op jit(solution)/shard_map/all_to_all | solution.py:20
  100.0 8.6 %all-to-all-done.3 = f32[16,4,128]{2,1,0:T(4,128)S(1)} async-done(((f32[16,4,128]{2,1,0:T(4,128)}), f32[16,4,128]{2,1,0:T(4,128)S(1)}, u32[]{:S(2)}, u32[]{:S(2)}) %all-to-all-start.3) | async-done | bytes 32800 | tf_op jit(solution)/shard_map/all_to_all | solution.py:20
  108.7 0.1 fusion.57
  108.7 0.7 fusion.54
  111.0 0.1 reshape.159
  111.1 3.5 %add.69 = f32[384,2304]{1,0:T(8,128)S(1)} add(f32[384,2304]{1,0:T(8,128)} %convolution_add_fusion.1, f32[384,2304]{1,0:T(8,128)} %collective-permute-done.4) | non-fusion elementwise | flops 884736 | bytes 10616832 | tf_op jit(solution)/shard_map/add | solution.py:163
  114.6 0.4 fusion.12
  115.0 17.1 %all_to_all.31.parts_ref = bf16[4,48,2304]{2,1,0:T(8,128)(2,1)} all-to-all(bf16[4,48,2304]{2,1,0:T(8,128)(2,1)S(1)} %bitcast.70), channel_id=1, replica_groups=mesh['x'=4,'yh'=2,'c'=2,'yl'=4,'z'=8] {'x'}, dimensions={0} | all-to-all | bytes 1769472 | tf_op jit(solution)/shard_map/all_to_all | solution.py:191
  132.2 2.1 %shard_map.60 = bf16[64,16,128]{2,1,0:T(8,128)(2,1)} custom-call(bf16[4,48,2304]{2,1,0:T(8,128)(2,1)} %all_to_all.31.parts_ref), custom_call_target="tpu_custom_call" | custom-call | tf_op jit(solution)/shard_map/pallas_call | solution.py:75
  134.3 9.6 %all-to-all-start.5 = ((bf16[64,16,128]{2,1,0:T(8,128)(2,1)}), bf16[64,16,128]{2,1,0:T(8,128)(2,1)S(1)}, u32[]{:S(2)}, u32[]{:S(2)}) async-start(bf16[64,16,128]{2,1,0:T(8,128)(2,1)} %shard_map.60), calls=%async_computation.5 | async-start | bytes 524288 | tf_op jit(solution)/shard_map/all_to_all | solution.py:192
  144.1 1.4 fusion.34
  145.5 4.3 %fusion = bf16[2304,1,1,512]{3,0,2,1:T(8,128)(2,1)} fusion(bf16[192,2304]{1,0:T(8,128)(2,1)} %copy-done.9, bf16[192,2304]{1,0:T(8,128)(2,1)} %copy-done.8, bf16[192,512]{1,0:T(8,128)(2,1)S(1)} %get-tuple-element.15, bf16[192,512]{1,0:T(8,128)(2,1)S(1)} %get-tuple-element.14), kind=kOutput, calls=%fused_computation.3 | convolution fusion | flops 911474688 | bytes 4521984 | tf_op jit(solution)/shard_map/dot_general | solution.py:183
  149.8 8.6 %all-to-all-done.5.parts_ref = bf16[64,16,128]{2,1,0:T(8,128)(2,1)S(1)} async-done(((bf16[64,16,128]{2,1,0:T(8,128)(2,1)}), bf16[64,16,128]{2,1,0:T(8,128)(2,1)S(1)}, u32[]{:S(2)}, u32[]{:S(2)}) %all-to-all-start.5) | async-done | bytes 262176 | tf_op jit(solution)/shard_map/all_to_all | solution.py:192
  158.4 0.7 copy-done.7
  159.1 1.7 %shard_map.61 = bf16[24,72]{1,0:T(8,128)(2,1)} custom-call(bf16[64,16,128]{2,1,0:T(8,128)(2,1)} %copy-done.7), custom_call_target="tpu_custom_call" | custom-call | tf_op jit(solution)/shard_map/pallas_call | solution.py:87
  (46 shorter events, 1.0 us)
Async XLA Ops:
  0.6 62.9 %copy-start = (bf16[2304,1,1,512]{3,0,2,1:T(8,128)(2,1)S(1)}, bf16[2304,1,1,512]{3,0,2,1:T(8,128)(2,1)}, u32[]{:S(2)}) copy-start(bf16[2304,1,1,512]{3,0,2,1:T(8,128)(2,1)} %param.7) | copy-start | bytes 7077892
  3.6 31.2 %collective-permute-start = (bf16[4,24,512]{2,1,0:T(8,128)(2,1)}, bf16[4,24,512]{2,1,0:T(8,128)(2,1)S(1)}, u32[]{:S(2)}, u32[]{:S(2)}) collective-permute-start(bf16[4,24,512]{2,1,0:T(8,128)(2,1)} %bitcast.63), channel_id=1, source_target_pairs={{0,64},{32,96},{64,0},{96,32},{1,65},{33,97},{65,1},{97,33},{2,66}... | collective-permute-start | bytes 294920 | tf_op jit(solution)/shard_map/ppermute | solution.py:110
  12.8 26.4 %all-to-all-start = ((bf16[64,16,128]{2,1,0:T(8,128)(2,1)}), bf16[64,16,128]{2,1,0:T(8,128)(2,1)S(1)}, u32[]{:S(2)}, u32[]{:S(2)}) async-start(bf16[64,16,128]{2,1,0:T(8,128)(2,1)} %shard_map.59), calls=%async_computation | async-start | bytes 524288 | tf_op jit(solution)/shard_map/all_to_all | solution.py:97
  25.2 9.7 %collective-permute-start.1 = (bf16[4,24,512]{2,1,0:T(8,128)(2,1)}, bf16[4,24,512]{2,1,0:T(8,128)(2,1)S(1)}, u32[]{:S(2)}, u32[]{:S(2)}) collective-permute-start(bf16[4,24,512]{2,1,0:T(8,128)(2,1)} %bitcast.62), channel_id=1, source_target_pairs={{0,32},{32,0},{64,96},{96,64},{1,33},{33,1},{65,97},{97,65},{2,34}... | collective-permute-start | bytes 294920 | tf_op jit(solution)/shard_map/ppermute | solution.py:110
  27.2 10.6 %collective-permute-start.2 = (bf16[4,24,512]{2,1,0:T(8,128)(2,1)S(1)}, bf16[4,24,512]{2,1,0:T(8,128)(2,1)}, u32[]{:S(2)}, u32[]{:S(2)}) collective-permute-start(bf16[4,24,512]{2,1,0:T(8,128)(2,1)S(1)} %bitcast.74), channel_id=1, source_target_pairs={{0,96},{32,64},{64,32},{96,0},{1,97},{33,65},{65,33},{97,1},{2,98}... | collective-permute-start | bytes 294920 | tf_op jit(solution)/shard_map/ppermute | solution.py:110
  40.3 23.0 %copy-start.10 = (s32[24]{0:T(128)S(1)}, s32[24]{0:T(128)}, u32[]{:S(2)}) copy-start(s32[24]{0:T(128)} %param.5) | copy-start | bytes 292
  40.3 23.0 %copy-start.3 = (bf16[24,8192]{1,0:T(8,128)(2,1)S(1)}, bf16[24,8192]{1,0:T(8,128)(2,1)}, u32[]{:S(2)}) copy-start(bf16[24,8192]{1,0:T(8,128)(2,1)} %param.6) | copy-start | bytes 1179652
  61.3 4.4 %copy-start.1 = (bf16[4,48,3328]{2,1,0:T(8,128)(2,1)}, bf16[4,48,3328]{2,1,0:T(8,128)(2,1)S(1)}, u32[]{:S(2)}) copy-start(bf16[4,48,3328]{2,1,0:T(8,128)(2,1)S(1)} %all_to_all.30) | copy-start | bytes 3833860
  61.3 2.8 %copy-start.8 = (bf16[192,2304]{1,0:T(8,128)(2,1)}, bf16[192,2304]{1,0:T(8,128)(2,1)S(1)}, u32[]{:S(2)}) copy-start(bf16[192,2304]{1,0:T(8,128)(2,1)S(1)} %slice.102) | copy-start | bytes 2654212
  61.4 4.3 %collective-permute-start.3 = (bf16[192,2304]{1,0:T(8,128)(2,1)S(1)}, bf16[192,2304]{1,0:T(8,128)(2,1)S(1)}, u32[]{:S(2)}, u32[]{:S(2)}) collective-permute-start(bf16[192,2304]{1,0:T(8,128)(2,1)S(1)} %slice.102), channel_id=1, source_target_pairs={{0,32},{32,0},{1,33},{33,1},{2,34},{34,2},{3,35},{35,3},{4,36},{36... | collective-permute-start | bytes 2654216 | tf_op jit(solution)/shard_map/ppermute | solution.py:124
  64.2 3.2 %copy-start.4 = (f32[192,512]{1,0:T(8,128)}, f32[192,512]{1,0:T(8,128)S(1)}, u32[]{:S(2)}) copy-start(f32[192,512]{1,0:T(8,128)S(1)} %fusion.19) | copy-start | bytes 1179652
  65.7 1.7 %copy-start.9 = (bf16[192,2304]{1,0:T(8,128)(2,1)}, bf16[192,2304]{1,0:T(8,128)(2,1)S(1)}, u32[]{:S(2)}) copy-start(bf16[192,2304]{1,0:T(8,128)(2,1)S(1)} %collective-permute-done.3) | copy-start | bytes 2654212
  68.1 21.5 %all-to-all-start.2 = ((f32[32,4,128]{2,1,0:T(4,128)}), f32[32,4,128]{2,1,0:T(4,128)}, u32[]{:S(2)}, u32[]{:S(2)}) async-start(f32[32,4,128]{2,1,0:T(4,128)} %broadcast_in_dim.20), calls=%async_computation.2 | async-start | bytes 131072 | tf_op jit(solution)/shard_map/all_to_all | solution.py:20
  79.2 2.2 %copy-start.2 = (f32[192,512]{1,0:T(8,128)S(1)}, f32[192,512]{1,0:T(8,128)}, u32[]{:S(2)}) copy-start(f32[192,512]{1,0:T(8,128)} %get-tuple-element.20) | copy-start | bytes 1179652
  90.5 20.6 %collective-permute-start.4 = (f32[384,2304]{1,0:T(8,128)}, f32[384,2304]{1,0:T(8,128)}, u32[]{:S(2)}, u32[]{:S(2)}) collective-permute-start(f32[384,2304]{1,0:T(8,128)} %convolution_add_fusion), channel_id=1, source_target_pairs={{0,32},{32,0},{1,33},{33,1},{2,34},{34,2},{3,35},{35,3},{4,36},{36... | collective-permute-start | bytes 10616840 | tf_op jit(solution)/shard_map/ppermute | solution.py:163
  93.0 15.6 %all-to-all-start.3 = ((f32[16,4,128]{2,1,0:T(4,128)}), f32[16,4,128]{2,1,0:T(4,128)S(1)}, u32[]{:S(2)}, u32[]{:S(2)}) async-start(f32[16,4,128]{2,1,0:T(4,128)} %broadcast_in_dim.44), calls=%async_computation.3 | async-start | bytes 65536 | tf_op jit(solution)/shard_map/all_to_all | solution.py:20
  115.0 29.1 %copy-start.5 = (f32[192,512]{1,0:T(8,128)S(1)}, f32[192,512]{1,0:T(8,128)}, u32[]{:S(2)}) copy-start(f32[192,512]{1,0:T(8,128)} %copy-done.4) | copy-start | bytes 1179652
  115.0 29.0 %copy-start.6 = (f32[192,512]{1,0:T(8,128)S(1)}, f32[192,512]{1,0:T(8,128)}, u32[]{:S(2)}) copy-start(f32[192,512]{1,0:T(8,128)} %get-tuple-element.38) | copy-start | bytes 1179652
  134.3 24.1 %all-to-all-start.5 = ((bf16[64,16,128]{2,1,0:T(8,128)(2,1)}), bf16[64,16,128]{2,1,0:T(8,128)(2,1)S(1)}, u32[]{:S(2)}, u32[]{:S(2)}) async-start(bf16[64,16,128]{2,1,0:T(8,128)(2,1)} %shard_map.60), calls=%async_computation.5 | async-start | bytes 524288 | tf_op jit(solution)/shard_map/all_to_all | solution.py:192
  158.4 0.7 copy-start.7

commit v2 on v0

v2 whole, which is shorter than its diff:
```python
import jax
import jax.numpy as jnp
from jax import lax
from jax.experimental import pallas as pl
from jax.experimental.pallas import tpu as pltpu
from jax.sharding import Mesh
from jax.sharding import PartitionSpec as P

SIZES = {"x": 4, "yh": 2, "c": 2, "yl": 4, "z": 8}
SEQ = ("x", "yh", "c")
VOCAB = ("yl", "z")
PLANE = ("yh", "yl", "z")
SWAP = [(0, 1), (1, 0)]
f32, bf16 = jnp.float32, jnp.bfloat16


KERNEL = pltpu.CompilerParams(vmem_limit_bytes=24 * 1024 * 1024)
IN_HBM = pl.BlockSpec(memory_space=pltpu.HBM)
IN_VMEM = pl.BlockSpec(memory_space=pltpu.VMEM)
HELD = (4, 2304, 256)


def in_hbm(array):
    return pltpu.with_memory_space_constraint(array, pltpu.HBM)


def logits_kernel(
    got_ref, own_ref, far_ref, extra_ref, exp_ref, slope_ref, stats_ref, give_ref, held, sems
):
    copies = []
    for at in range(4):
        source = (own_ref, far_ref)[at // 2].at[:, pl.ds(256 * (at % 2), 256)]
        copies.append(pltpu.make_async_copy(source, held.at[at], sems.at[at]))
        copies[at].start()
    depth = own_ref.shape[0]
    rows = jnp.concatenate([got_ref[at, :, :depth] for at in range(4)], axis=0)
    for at in range(4):
        give_ref[at] = got_ref[at, :, depth:].astype(f32)[24:].astype(bf16)
    sums = jnp.zeros((192, 1), f32)
    for at in range(4):
        copies[at].wait()
        logits = jnp.dot(rows, held[at], preferred_element_type=f32)
        capped_tanh = jnp.tanh(logits / 30.0)
        exp_logits = jnp.exp(30.0 * capped_tanh)
        columns = slice(256 * at, 256 * at + 256)
        exp_ref[:, columns] = exp_logits
        slope_ref[:, columns] = 1.0 - capped_tanh * capped_tanh
        sums = sums + jnp.sum(exp_logits, axis=1, keepdims=True)
    wide = jnp.broadcast_to(sums, (192, 128))
    first = jnp.transpose(wide[:128])[:1]
    last = jnp.transpose(jnp.concatenate([wide[128:], jnp.zeros((64, 128), f32)], axis=0))[:1]
    lane = lax.broadcasted_iota(jnp.int32, (1, 128), 1)
    stats = jnp.concatenate([first, jnp.where(lane < 64, last, extra_ref[...])], axis=0)
    stats_ref[...] = jnp.broadcast_to(stats[None], stats_ref.shape)


def logits_of(got, own, far, extra):
    wide = jax.ShapeDtypeStruct((192, 1024), f32)
    stats = jax.ShapeDtypeStruct((64, 2, 128), f32)
    return pl.pallas_call(
        logits_kernel,
        in_specs=[IN_VMEM, IN_HBM, IN_HBM, IN_VMEM],
        out_shape=(wide, wide, stats, jax.ShapeDtypeStruct((4, 24, 1024), bf16)),
        scratch_shapes=[pltpu.VMEM(HELD, bf16), pltpu.SemaphoreType.DMA((4,))],
        compiler_params=KERNEL,
    )(got, in_hbm(own), in_hbm(far), extra)


def stats_kernel(stats_ref, out_ref):
    first = stats_ref[0, :1, :]
    for at in range(1, 64):
        first = first + stats_ref[at, :1, :]
    halves = []
    for y_at in range(2):
        total = stats_ref[32 * y_at, 1:, :]
        for at in range(1, 32):
            total = total + stats_ref[32 * y_at + at, 1:, :]
        halves.append(total)
    lane = lax.broadcasted_iota(jnp.int32, (1, 128), 1)
    low = jnp.where(lane < 88, halves[0], stats_ref[0, 1:, :])
    high = jnp.where(lane < 88, halves[1], stats_ref[32, 1:, :])
    low = jnp.where(lane < 64, halves[0] + halves[1], low)
    rows = jnp.concatenate([first, low, high, high], axis=0)
    out_ref[...] = jnp.broadcast_to(rows[None], out_ref.shape)


def stats_over_plane(stats):
    out = jax.ShapeDtypeStruct((4, 4, 128), f32)
    return pl.pallas_call(stats_kernel, out_shape=out)(stats)


def grads_kernel(
    stats_ref,
    exp_ref,
    slope_ref,
    target_ref,
    own_ref,
    far_ref,
    part_ref,
    grad_own_ref,
    grad_far_ref,
    held,
    made,
    sems,
    out_sems,
):
    copies = []
    for at in range(4):
        source = (own_ref, far_ref)[at % 2].at[pl.ds(1152 * (at // 2), 1152), :]
        copies.append(pltpu.make_async_copy(source, held.at[at], sems.at[at]))
        copies[at].start()
    firsts = [stats_ref[at, :1, :] for at in range(4)]
    seconds = [stats_ref[at // 2, 1 + at % 2 : 2 + at % 2, :] for at in range(8)]
    rows = jnp.concatenate([sum(firsts), sum(seconds[::2])] + seconds, axis=0)
    lane = lax.broadcasted_iota(jnp.int32, (1, 128), 1)
    counted = jnp.where((lane >= 88) & (lane < 113), sum(seconds), 0.0)
    factor = 8.0 * 262144 / jnp.sum(counted, axis=1, keepdims=True)
    columns = jnp.transpose(jnp.concatenate([rows, jnp.zeros((118, 128), f32)], axis=0))
    sum_exp = jnp.concatenate([columns[:, 0:1], columns[:64, 1:2]], axis=0)
    mass = jnp.concatenate([columns[64:88, 2 + at : 3 + at] for at in range(8)], axis=0)
    mask = jnp.concatenate([columns[88:112, 2 + at : 3 + at] for at in range(8)], axis=0)
    scale, share = factor * mask, mass / sum_exp
    grads = []
    for half_at, grad_ref in enumerate((grad_own_ref, grad_far_ref)):
        entries = slice(512 * half_at, 512 * half_at + 512)
        grad = scale * (exp_ref[:, entries] * share - target_ref[:, entries].astype(f32))
        grad = (grad * slope_ref[:, entries]).astype(bf16)
        grad_ref[...] = grad
        grads.append(grad)
    dims = (((1,), (1,)), ((), ()))
    sent = []
    for half_at in range(2):
        copies[2 * half_at].wait()
        copies[2 * half_at + 1].wait()
        for start in range(0, 1152, 384):
            block = slice(start, start + 384)
            part = lax.dot_general(
                grads[0], held[2 * half_at, block, :], dims, preferred_element_type=f32
            ) + lax.dot_general(
                grads[1], held[2 * half_at + 1, block, :], dims, preferred_element_type=f32
            )
            part = part.astype(bf16)
            for at in range(4):
                made[half_at, at, :, block] = part[48 * at : 48 * at + 48]
        target = part_ref.at[:, :, pl.ds(1152 * half_at, 1152)]
        sent.append(pltpu.make_async_copy(made.at[half_at], target, out_sems.at[half_at]))
        sent[half_at].start()
    for copy in sent:
        copy.wait()


def grads_of(stats, exp_logits, slope, target, own, far):
    grad = pltpu.HBM((192, 512), bf16)
    return pl.pallas_call(
        grads_kernel,
        in_specs=[IN_VMEM] * 4 + [IN_HBM] * 2,
        out_specs=(IN_HBM, IN_VMEM, IN_VMEM),
        out_shape=(pltpu.HBM((4, 48, own.shape[0]), bf16), grad, grad),
        scratch_shapes=[
            pltpu.VMEM((4, 1152, 512), bf16),
            pltpu.VMEM((2, 4, 48, 1152), bf16),
            pltpu.SemaphoreType.DMA((4,)),
            pltpu.SemaphoreType.DMA((2,)),
        ],
        compiler_params=KERNEL,
    )(stats, exp_logits, slope, target, in_hbm(own), in_hbm(far))


def packed(block):
    first, second, third = block[:8], block[8:16], block[16:]
    top = jnp.concatenate([first, second[:, :56]], axis=1)
    rest = jnp.concatenate([second[:, 56:], third, jnp.zeros((8, 40), block.dtype)], axis=1)
    return jnp.concatenate([top, rest], axis=0)


def unpacked(block):
    top, rest = block[..., :8, :], block[..., 8:, :]
    second = jnp.concatenate([top[..., 72:], rest[..., :16]], axis=-1)
    return jnp.concatenate([top[..., :72], second, rest[..., 16:88]], axis=-2)


def pack_copies_kernel(block_ref, out_ref):
    block = packed(block_ref[...].astype(f32)).astype(bf16)
    out_ref[...] = jnp.broadcast_to(block[None], out_ref.shape)


def pack_copies(block):
    out = jax.ShapeDtypeStruct((64, 16, 128), bf16)
    return pl.pallas_call(pack_copies_kernel, out_shape=out)(block)


def sum_pack_kernel(parts_ref, out_ref, held, sems):
    copies = []
    for at in range(2):
        source = parts_ref.at[:, :, pl.ds(1152 * at, 1152)]
        copies.append(pltpu.make_async_copy(source, held.at[at], sems.at[at]))
        copies[at].start()
    for at in range(2):
        copies[at].wait()
        total = held[at, 0].astype(f32)
        for x_at in range(1, 4):
            total = total + held[at, x_at].astype(f32)
        for shard in range(16):
            columns = total[:, 72 * shard : 72 * shard + 72]
            for y_at in range(2):
                block = packed(columns[24 * y_at : 24 * y_at + 24])
                out_ref[32 * y_at + 16 * at + shard] = block.astype(bf16)


def sum_pack(parts):
    return pl.pallas_call(
        sum_pack_kernel,
        in_specs=[IN_HBM],
        out_shape=jax.ShapeDtypeStruct((64, 16, 128), bf16),
        scratch_shapes=[pltpu.VMEM((2, 4, 48, 1152), bf16), pltpu.SemaphoreType.DMA((2,))],
        compiler_params=KERNEL,
    )(parts)


def shards(hidden_states, loss_mask, teacher_probs, head_weight):
    tokens, features = hidden_states.shape
    feature_dim, shard_cols = head_weight.shape[0], head_weight.shape[3]
    half = 8 * tokens
    weight = head_weight.reshape(feature_dim, shard_cols)
    y_at, core = lax.axis_index("yh"), lax.axis_index("c")

    copies, weight, teacher_probs, loss_mask = lax.optimization_barrier(
        (pack_copies(hidden_states), weight, teacher_probs, loss_mask)
    )
    plane = unpacked(lax.all_to_all(copies, PLANE, 0, 0, tiled=True))
    plane = plane.reshape(2, 32, tokens, features)
    rows = plane.transpose(0, 2, 1, 3).reshape(2 * tokens, feature_dim)

    weight_other = lax.ppermute(weight, "c", SWAP)
    mask_mine = loss_mask.astype(f32)
    mask_other = lax.ppermute(mask_mine, "c", SWAP)
    mass_part = jnp.sum(teacher_probs.astype(f32), axis=1)

    by_owner = teacher_probs.reshape(tokens, 4, 2, 2, shard_cols)


    def entries(far_y, far_core):
        at_zero, at_one = (
            jnp.where((core == 0) != far_core, by_owner[:, :, at, 0], by_owner[:, :, at, 1])
            for at in range(2)
        )
        return jnp.where((y_at == 0) != far_y, at_zero, at_one).transpose(1, 0, 2)

    by_owner = jnp.concatenate(
        [
            jnp.concatenate([entries(far_y, far_core) for far_core in (False, True)], axis=2)
            for far_y in (False, True)
        ],
        axis=1,
    )

    blank = half - 128
    extra = jnp.concatenate(
        [
            jnp.zeros((blank,), f32),
            mass_part,
            mask_mine,
            jnp.sum(mask_other, keepdims=True),
            jnp.zeros((128 - blank - 2 * tokens - 1,), f32),
        ]
    )

    sent = jnp.concatenate([jnp.broadcast_to(rows[None], (4,) + rows.shape), by_owner], axis=2)
    sent, extra = lax.optimization_barrier((sent, extra))
    got = lax.all_to_all(sent, "x", 0, 0, tiled=True)

    exp_logits, slope, stats, give = logits_of(got, weight, weight_other, extra[None])
    stats = stats_over_plane(lax.all_to_all(stats, PLANE, 0, 0, tiled=True))
    stats = lax.all_to_all(stats, "x", 0, 0, tiled=True)

    kept, came = got[:, :tokens, feature_dim:], lax.ppermute(give, "yh", SWAP)
    low, high = jnp.where(y_at == 0, kept, came), jnp.where(y_at == 0, came, kept)
    target = jnp.stack([low, high], axis=1).reshape(half, 2 * shard_cols)

    stats, target = lax.optimization_barrier((stats, target))
    part, grad_own, grad_far = grads_of(stats, exp_logits, slope, target, weight, weight_other)
    mine = got[:, :, :feature_dim].reshape(half, feature_dim)

    states = jnp.concatenate([mine, lax.ppermute(mine, "c", SWAP)])
    grad_logits = jnp.concatenate([grad_own, lax.ppermute(grad_far, "c", SWAP)])
    head_grad = lax.dot_general(
        states, grad_logits, (((0,), (0,)), ((), ())), preferred_element_type=f32
    )
    grad_head = head_grad.astype(bf16).reshape(head_weight.shape)

    part = sum_pack(lax.all_to_all(part, "x", 0, 0, tiled=True))
    part = lax.all_to_all(part, PLANE, 0, 0, tiled=True)
    grad_hidden = unpacked(jnp.sum(part.astype(f32), axis=0)).astype(bf16)
    return grad_hidden, grad_head


def solution(mesh):
    fine = Mesh(mesh.devices.reshape(tuple(SIZES.values())), tuple(SIZES))
    head = P(None, VOCAB, SEQ, None)
    return jax.shard_map(
        shards,
        mesh=fine,
        in_specs=(P(SEQ, VOCAB), P(SEQ), P(SEQ, VOCAB), head),
        out_specs=(P(SEQ, VOCAB), head),
        check_vma=False,
    )
```

time: 511 us -> 131 us (0.26)
  the two profiles are of different devices: /device:TPU:64 before, /device:TPU:2 now
where the time goes in v2:
time: 131 us
  starting transfers between devices  44.5 us (34%)
  blocking collectives  37.2 us (28%)
  waiting for transfers between devices  25.5 us (19%)
  Pallas kernels  13.5 us (10%)
  local copies, waits for them, and re-layouts  3.62 us (3%)
  matrix products  2.83 us (2%)
  other arithmetic  2.75 us (2%)
    all_to_all x1, blocking collectives, shards(): stats = stats_over_plane(lax.all_to_all(stats, PLANE, 0, 0, tiled=True))  19.1 us
    all_to_all x1, blocking collectives, shards(): got = lax.all_to_all(sent, 'x', 0, 0, tiled=True)  18 us
    all_to_all x1, starting transfers between devices, shards(): plane = unpacked(lax.all_to_all(copies, PLANE, 0, 0, tiled=True))  16.7 us
    all_to_all x1, waiting for transfers between devices, shards(): part = lax.all_to_all(part, PLANE, 0, 0, tiled=True)  7.49 us
    all_to_all x1, waiting for transfers between devices, shards(): part = sum_pack(lax.all_to_all(part, 'x', 0, 0, tiled=True))  6.57 us
    all_to_all x1, waiting for transfers between devices, shards(): plane = unpacked(lax.all_to_all(copies, PLANE, 0, 0, tiled=True))  6.32 us
    ppermute x1, starting transfers between devices, shards(): kept, came = (got[:, :tokens, feature_dim:], lax.ppermute(give, 'yh', SWAP))  5.29 us
    pallas_call x1, Pallas kernels, grads_of(): pl.pallas_call(grads_kernel, in_specs=[IN_VMEM] * 4 + [IN_HBM] * 2, out_s...  5.21 us
  transfers between devices with their start and end apart: 9, of which 5 were waited for; matrix products, arithmetic and copies ran while one was open for 6% of the time, Pallas kernels for 2%

profile of v2, /device:TPU:2, one launch (start us, length us, event | category | flops | bytes accessed | tf_op | source)
XLA Modules:
  0.0 130.8 jit_solution(16505800071141868035)
XLA Ops:
  0.6 1.5 %shard_map.59 = bf16[64,16,128]{2,1,0:T(8,128)(2,1)} custom-call(bf16[24,72]{1,0:T(8,128)(2,1)} %block_ref.1), custom_call_target="tpu_custom_call" | custom-call | tf_op jit(solution)/shard_map/pallas_call | solution.py:189
  2.1 16.7 %all-to-all-start = ((bf16[64,16,128]{2,1,0:T(8,128)(2,1)}), bf16[64,16,128]{2,1,0:T(8,128)(2,1)S(1)}, u32[]{:S(2)}, u32[]{:S(2)}) async-start(bf16[64,16,128]{2,1,0:T(8,128)(2,1)} %shard_map.59), calls=%async_computation | async-start | bytes 524288 | tf_op jit(solution)/shard_map/all_to_all | solution.py:230
  18.8 0.7 convert_element_type.14
  19.5 1.9 %collective-permute-start = (f32[24]{0:T(128)S(1)}, f32[24]{0:T(128)S(1)}, u32[]{:S(2)}, u32[]{:S(2)}) collective-permute-start(f32[24]{0:T(128)S(1)} %convert_element_type.14), channel_id=1, source_target_pairs={{0,32},{32,0},{1,33},{33,1},{2,34},{34,2},{3,35},{35,3},{4,36},{36... | collective-permute-start | bytes 296 | tf_op jit(solution)/shard_map/ppermute | solution.py:236
  21.4 2.4 %collective-permute-start.1 = (bf16[2304,512]{1,0:T(8,128)(2,1)}, bf16[2304,512]{1,0:T(8,128)(2,1)}, u32[]{:S(2)}, u32[]{:S(2)}) collective-permute-start(bf16[2304,512]{1,0:T(8,128)(2,1)} %bitcast.34), channel_id=1, source_target_pairs={{0,32},{32,0},{1,33},{33,1},{2,34},{34,2},{3,35},{35,3},{4,36},{36... | collective-permute-start | bytes 7077896 | tf_op jit(solution)/shard_map/ppermute | solution.py:234
  23.8 1.3 reshape.41
  25.1 0.5 fusion.8
  25.7 0.2 select_bitcast_fusion.5
  26.0 0.0 copy-done
  26.0 0.2 convert_reduce_fusion
  26.2 0.0 collective-permute-done
  26.2 0.6 reduce_sum.28
  26.8 0.7 concatenate.41
  27.5 6.3 %all-to-all-done = bf16[64,16,128]{2,1,0:T(8,128)(2,1)S(1)} async-done(((bf16[64,16,128]{2,1,0:T(8,128)(2,1)}), bf16[64,16,128]{2,1,0:T(8,128)(2,1)S(1)}, u32[]{:S(2)}, u32[]{:S(2)}) %all-to-all-start) | async-done | bytes 262176 | tf_op jit(solution)/shard_map/all_to_all | solution.py:230
  33.8 0.1 slice.85
  34.0 0.1 fusion.9
  34.1 0.1 pad_maximum_fusion
  34.2 0.1 copy.8
  34.3 0.5 broadcast_in_dim.16
  34.7 0.1 broadcast_in_dim.17
  34.8 0.1 maximum_maximum_fusion
  34.9 18.0 %all_to_all.30.got_ref = bf16[4,48,3328]{2,1,0:T(8,128)(2,1)S(1)} all-to-all(bf16[4,48,3328]{2,1,0:T(8,128)(2,1)S(1)} %maximum_maximum_fusion), channel_id=1, replica_groups=mesh['x'=4,'yh'=2,'c'=2,'yl'=4,'z'=8] {'x'}, dimensions={0} | all-to-all | bytes 2555904 | tf_op jit(solution)/shard_map/all_to_all | solution.py:270
  52.9 0.0 collective-permute-done.1.far_ref
  52.9 4.2 %shard_map.60 = (f32[192,1024]{1,0:T(8,128)S(1)}, f32[192,1024]{1,0:T(8,128)S(1)}, f32[64,2,128]{2,1,0:T(2,128)S(1)}, bf16[4,24,1024]{2,1,0:T(8,128)(2,1)S(1)}) custom-call(bf16[4,48,3328]{2,1,0:T(8,128)(2,1)S(1)} %all_to_all.30.got_ref, bf16[2304,512]{1,0:T(8,128)(2,1)} %bitcast.35, bf16[2304,512]{1,0:T(8,128)(2,1)} %collective-permute-done.1.far_ref, ...), custom_call_target="tpu_custom_call" | custom-call | tf_op jit(solution)/shard_map/pallas_call | solution.py:60
  57.1 5.3 %collective-permute-start.2 = (bf16[4,24,1024]{2,1,0:T(8,128)(2,1)S(1)}, bf16[4,24,1024]{2,1,0:T(8,128)(2,1)S(1)}, u32[]{:S(2)}, u32[]{:S(2)}) collective-permute-start(bf16[4,24,1024]{2,1,0:T(8,128)(2,1)S(1)} %get-tuple-element.24), channel_id=1, source_target_pairs={{0,64},{64,0},{1,65},{65,1},{2,66},{66,2},{3,67},{67,3},{4,68},{68... | collective-permute-start | bytes 589832 | tf_op jit(solution)/shard_map/ppermute | solution.py:276
  62.4 19.1 %all_to_all.31.stats_ref = f32[64,2,128]{2,1,0:T(2,128)} all-to-all(f32[64,2,128]{2,1,0:T(2,128)S(1)} %get-tuple-element.23), channel_id=1, replica_groups=mesh['x'=4,'yh'=2,'c'=2,'yl'=4,'z'=8] {'yh','yl','z'}, dimensions={0} | all-to-all | bytes 131072 | tf_op jit(solution)/shard_map/all_to_all | solution.py:273
  81.5 1.5 %shard_map.61 = f32[4,4,128]{2,1,0:T(4,128)} custom-call(f32[64,2,128]{2,1,0:T(2,128)} %all_to_all.31.stats_ref), custom_call_target="tpu_custom_call" | custom-call | tf_op jit(solution)/shard_map/pallas_call | solution.py:89
  83.1 4.7 %all-to-all-start.3 = ((f32[4,4,128]{2,1,0:T(4,128)}), f32[4,4,128]{2,1,0:T(4,128)S(1)}, u32[]{:S(2)}, u32[]{:S(2)}) async-start(f32[4,4,128]{2,1,0:T(4,128)} %shard_map.61), calls=%async_computation.3 | async-start | bytes 16384 | tf_op jit(solution)/shard_map/all_to_all | solution.py:274
  87.7 0.0 collective-permute-done.2
  87.9 3.7 %all-to-all-done.3.stats_ref = f32[4,4,128]{2,1,0:T(4,128)S(1)} async-done(((f32[4,4,128]{2,1,0:T(4,128)}), f32[4,4,128]{2,1,0:T(4,128)S(1)}, u32[]{:S(2)}, u32[]{:S(2)}) %all-to-all-start.3) | async-done | bytes 8224 | tf_op jit(solution)/shard_map/all_to_all | solution.py:274
  91.6 5.2 %shard_map.62 = (bf16[4,48,2304]{2,1,0:T(8,128)(2,1)}, bf16[192,512]{1,0:T(8,128)(2,1)}, bf16[192,512]{1,0:T(8,128)(2,1)}) custom-call(f32[4,4,128]{2,1,0:T(4,128)S(1)} %all-to-all-done.3.stats_ref, f32[192,1024]{1,0:T(8,128)S(1)} %get-tuple-element.26.exp_ref, f32[192,1024]{1,0:T(8,128)S(1)} %get-tuple-element.27.slope_ref, bf16[192,1024]{1,0:T(8,128)(2,1)S(1)} %bitcast.32, ...), custom_call_target="tpu_custom_call" | custom-call | tf_op jit(solution)/shard_map/pallas_call | solution.py:154
  96.8 0.0 copy-start.2
  96.8 0.0 copy-start.1
  96.8 5.1 %all-to-all-start.4 = ((bf16[4,48,2304]{2,1,0:T(8,128)(2,1)}), bf16[4,48,2304]{2,1,0:T(8,128)(2,1)S(1)}, u32[]{:S(2)}, u32[]{:S(2)}) async-start(bf16[4,48,2304]{2,1,0:T(8,128)(2,1)} %get-tuple-element.29), calls=%async_computation.4 | async-start | bytes 1769472 | tf_op jit(solution)/shard_map/all_to_all | solution.py:291
  101.9 0.1 slice.97
  102.0 1.9 %collective-permute-start.3 = (bf16[192,2304]{1,0:T(8,128)(2,1)S(1)}, bf16[192,2304]{1,0:T(8,128)(2,1)S(1)}, u32[]{:S(2)}, u32[]{:S(2)}) collective-permute-start(bf16[192,2304]{1,0:T(8,128)(2,1)S(1)} %bitcast.38), channel_id=1, source_target_pairs={{0,32},{32,0},{1,33},{33,1},{2,34},{34,2},{3,35},{35,3},{4,36},{36... | collective-permute-start | bytes 2654216 | tf_op jit(solution)/shard_map/ppermute | solution.py:284
  103.9 6.6 %all-to-all-done.4.parts_ref = bf16[4,48,2304]{2,1,0:T(8,128)(2,1)S(1)} async-done(((bf16[4,48,2304]{2,1,0:T(8,128)(2,1)}), bf16[4,48,2304]{2,1,0:T(8,128)(2,1)S(1)}, u32[]{:S(2)}, u32[]{:S(2)}) %all-to-all-start.4) | async-done | bytes 884768 | tf_op jit(solution)/shard_map/all_to_all | solution.py:291
  110.5 1.1 shard_map.63
  111.6 4.6 %all-to-all-start.5 = ((bf16[64,16,128]{2,1,0:T(8,128)(2,1)}), bf16[64,16,128]{2,1,0:T(8,128)(2,1)S(1)}, u32[]{:S(2)}, u32[]{:S(2)}) async-start(bf16[64,16,128]{2,1,0:T(8,128)(2,1)} %shard_map.63), calls=%async_computation.5 | async-start | bytes 524288 | tf_op jit(solution)/shard_map/all_to_all | solution.py:292
  116.2 1.9 %collective-permute-start.4 = (bf16[192,512]{1,0:T(8,128)(2,1)S(1)}, bf16[192,512]{1,0:T(8,128)(2,1)S(1)}, u32[]{:S(2)}, u32[]{:S(2)}) collective-permute-start(bf16[192,512]{1,0:T(8,128)(2,1)S(1)} %copy-done.2), channel_id=1, source_target_pairs={{0,32},{32,0},{1,33},{33,1},{2,34},{34,2},{3,35},{35,3},{4,36},{36... | collective-permute-start | bytes 589832 | tf_op jit(solution)/shard_map/ppermute | solution.py:285
  118.1 0.0 collective-permute-done.3
  118.1 1.4 %collective-permute-done.4 = bf16[192,512]{1,0:T(8,128)(2,1)S(1)} collective-permute-done((bf16[192,512]{1,0:T(8,128)(2,1)S(1)}, bf16[192,512]{1,0:T(8,128)(2,1)S(1)}, u32[]{:S(2)}, u32[]{:S(2)}) %collective-permute-start.4) | collective-permute-done | bytes 196640 | tf_op jit(solution)/shard_map/ppermute | solution.py:285
  119.5 2.8 %fusion = bf16[2304,1,1,512]{3,0,2,1:T(8,128)(2,1)} fusion(bf16[192,2304]{1,0:T(8,128)(2,1)S(1)} %collective-permute-done.3, bf16[192,2304]{1,0:T(8,128)(2,1)S(1)} %bitcast.39, bf16[192,512]{1,0:T(8,128)(2,1)S(1)} %collective-permute-done.4, bf16[192,512]{1,0:T(8,128)(2,1)S(1)} %copy-done.1), kind=kOutput, calls=%fused_computation.1 | convolution fusion | flops 911474688 | bytes 4521984 | tf_op jit(solution)/shard_map/dot_general | solution.py:286
  122.4 7.5 %all-to-all-done.5 = bf16[64,16,128]{2,1,0:T(8,128)(2,1)S(1)} async-done(((bf16[64,16,128]{2,1,0:T(8,128)(2,1)}), bf16[64,16,128]{2,1,0:T(8,128)(2,1)S(1)}, u32[]{:S(2)}, u32[]{:S(2)}) %all-to-all-start.5) | async-done | bytes 262176 | tf_op jit(solution)/shard_map/all_to_all | solution.py:292
  129.9 0.1 reduce
  129.9 0.1 fusion.10
  130.0 0.1 slice.94
  130.1 0.7 pad_maximum_fusion.2
  (11 shorter events, 0.2 us)
Async XLA Ops:
  2.1 23.9 %copy-start = (bf16[24,8192]{1,0:T(8,128)(2,1)S(1)}, bf16[24,8192]{1,0:T(8,128)(2,1)}, u32[]{:S(2)}) copy-start(bf16[24,8192]{1,0:T(8,128)(2,1)} %param.6) | copy-start | bytes 1179652
  2.1 31.7 %all-to-all-start = ((bf16[64,16,128]{2,1,0:T(8,128)(2,1)}), bf16[64,16,128]{2,1,0:T(8,128)(2,1)S(1)}, u32[]{:S(2)}, u32[]{:S(2)}) async-start(bf16[64,16,128]{2,1,0:T(8,128)(2,1)} %shard_map.59), calls=%async_computation | async-start | bytes 524288 | tf_op jit(solution)/shard_map/all_to_all | solution.py:230
  19.5 6.7 %collective-permute-start = (f32[24]{0:T(128)S(1)}, f32[24]{0:T(128)S(1)}, u32[]{:S(2)}, u32[]{:S(2)}) collective-permute-start(f32[24]{0:T(128)S(1)} %convert_element_type.14), channel_id=1, source_target_pairs={{0,32},{32,0},{1,33},{33,1},{2,34},{34,2},{3,35},{35,3},{4,36},{36... | collective-permute-start | bytes 296 | tf_op jit(solution)/shard_map/ppermute | solution.py:236
  21.4 31.5 %collective-permute-start.1 = (bf16[2304,512]{1,0:T(8,128)(2,1)}, bf16[2304,512]{1,0:T(8,128)(2,1)}, u32[]{:S(2)}, u32[]{:S(2)}) collective-permute-start(bf16[2304,512]{1,0:T(8,128)(2,1)} %bitcast.34), channel_id=1, source_target_pairs={{0,32},{32,0},{1,33},{33,1},{2,34},{34,2},{3,35},{35,3},{4,36},{36... | collective-permute-start | bytes 7077896 | tf_op jit(solution)/shard_map/ppermute | solution.py:234
  57.1 30.6 %collective-permute-start.2 = (bf16[4,24,1024]{2,1,0:T(8,128)(2,1)S(1)}, bf16[4,24,1024]{2,1,0:T(8,128)(2,1)S(1)}, u32[]{:S(2)}, u32[]{:S(2)}) collective-permute-start(bf16[4,24,1024]{2,1,0:T(8,128)(2,1)S(1)} %get-tuple-element.24), channel_id=1, source_target_pairs={{0,64},{64,0},{1,65},{65,1},{2,66},{66,2},{3,67},{67,3},{4,68},{68... | collective-permute-start | bytes 589832 | tf_op jit(solution)/shard_map/ppermute | solution.py:276
  83.1 8.5 %all-to-all-start.3 = ((f32[4,4,128]{2,1,0:T(4,128)}), f32[4,4,128]{2,1,0:T(4,128)S(1)}, u32[]{:S(2)}, u32[]{:S(2)}) async-start(f32[4,4,128]{2,1,0:T(4,128)} %shard_map.61), calls=%async_computation.3 | async-start | bytes 16384 | tf_op jit(solution)/shard_map/all_to_all | solution.py:274
  96.8 19.4 %copy-start.2 = (bf16[192,512]{1,0:T(8,128)(2,1)S(1)}, bf16[192,512]{1,0:T(8,128)(2,1)}, u32[]{:S(2)}) copy-start(bf16[192,512]{1,0:T(8,128)(2,1)} %get-tuple-element.31) | copy-start | bytes 589828
  96.8 22.7 %copy-start.1 = (bf16[192,512]{1,0:T(8,128)(2,1)S(1)}, bf16[192,512]{1,0:T(8,128)(2,1)}, u32[]{:S(2)}) copy-start(bf16[192,512]{1,0:T(8,128)(2,1)} %get-tuple-element.30) | copy-start | bytes 589828
  96.8 13.6 %all-to-all-start.4 = ((bf16[4,48,2304]{2,1,0:T(8,128)(2,1)}), bf16[4,48,2304]{2,1,0:T(8,128)(2,1)S(1)}, u32[]{:S(2)}, u32[]{:S(2)}) async-start(bf16[4,48,2304]{2,1,0:T(8,128)(2,1)} %get-tuple-element.29), calls=%async_computation.4 | async-start | bytes 1769472 | tf_op jit(solution)/shard_map/all_to_all | solution.py:291
  102.0 16.2 %collective-permute-start.3 = (bf16[192,2304]{1,0:T(8,128)(2,1)S(1)}, bf16[192,2304]{1,0:T(8,128)(2,1)S(1)}, u32[]{:S(2)}, u32[]{:S(2)}) collective-permute-start(bf16[192,2304]{1,0:T(8,128)(2,1)S(1)} %bitcast.38), channel_id=1, source_target_pairs={{0,32},{32,0},{1,33},{33,1},{2,34},{34,2},{3,35},{35,3},{4,36},{36... | collective-permute-start | bytes 2654216 | tf_op jit(solution)/shard_map/ppermute | solution.py:284
  111.6 18.3 %all-to-all-start.5 = ((bf16[64,16,128]{2,1,0:T(8,128)(2,1)}), bf16[64,16,128]{2,1,0:T(8,128)(2,1)S(1)}, u32[]{:S(2)}, u32[]{:S(2)}) async-start(bf16[64,16,128]{2,1,0:T(8,128)(2,1)} %shard_map.63), calls=%async_computation.5 | async-start | bytes 524288 | tf_op jit(solution)/shard_map/all_to_all | solution.py:292
  116.2 3.3 %collective-permute-start.4 = (bf16[192,512]{1,0:T(8,128)(2,1)S(1)}, bf16[192,512]{1,0:T(8,128)(2,1)S(1)}, u32[]{:S(2)}, u32[]{:S(2)}) collective-permute-start(bf16[192,512]{1,0:T(8,128)(2,1)S(1)} %copy-done.2), channel_id=1, source_target_pairs={{0,32},{32,0},{1,33},{33,1},{2,34},{34,2},{3,35},{35,3},{4,36},{36... | collective-permute-start | bytes 589832 | tf_op jit(solution)/shard_map/ppermute | solution.py:285

commit v3 on v2

v3 whole, which is shorter than its diff:
```python
import jax
import jax.numpy as jnp
from jax import lax
from jax.experimental import pallas as pl
from jax.experimental.pallas import tpu as pltpu
from jax.sharding import Mesh
from jax.sharding import PartitionSpec as P

SIZES = {"x": 4, "yh": 2, "c": 2, "yl": 4, "z": 8}
SEQ = ("x", "yh", "c")
VOCAB = ("yl", "z")
PLANE = ("yh", "yl", "z")
SWAP = [(0, 1), (1, 0)]
f32, bf16 = jnp.float32, jnp.bfloat16


KERNEL = pltpu.CompilerParams(vmem_limit_bytes=24 * 1024 * 1024)
IN_HBM = pl.BlockSpec(memory_space=pltpu.HBM)
IN_VMEM = pl.BlockSpec(memory_space=pltpu.VMEM)
HELD = (2, 2304, 256)


def in_hbm(array):
    return pltpu.with_memory_space_constraint(array, pltpu.HBM)


def logits_kernel(
    got_ref,
    own_ref,
    far_ref,
    mass_ref,
    mask_ref,
    far_mask_ref,
    tanh_ref,
    stats_ref,
    held,
    made,
    sems,
    out_sems,
):
    copies = []
    for at in range(2):
        source = far_ref.at[:, pl.ds(256 * at, 256)]
        copies.append(pltpu.make_async_copy(source, held.at[at], sems.at[at]))
        copies[at].start()
    rows = jnp.concatenate([got_ref[at] for at in range(4)], axis=0)
    sums, sent = jnp.zeros((192, 1), f32), []
    for at in range(4):
        columns = slice(256 * at, 256 * at + 256)
        if at >= 2:
            copies[at - 2].wait()
        weight = own_ref[:, columns] if at < 2 else held[at - 2]
        logits = jnp.dot(rows, weight, preferred_element_type=f32)
        capped_tanh = jnp.tanh(logits * (1.0 / 30.0))
        made[at] = capped_tanh
        target = tanh_ref.at[:, pl.ds(256 * at, 256)]
        sent.append(pltpu.make_async_copy(made.at[at], target, out_sems.at[at]))
        sent[at].start()
        sums = sums + jnp.sum(jnp.exp(30.0 * capped_tanh), axis=1, keepdims=True)
    wide = jnp.broadcast_to(sums, (192, 128))
    first = jnp.transpose(wide[:128])[:1]
    last = jnp.concatenate([wide[128:], mass_ref[...], jnp.zeros((40, 128), f32)], axis=0)
    last = jnp.transpose(last)[:1]
    count = jnp.sum(far_mask_ref[...], axis=1, keepdims=True)
    blank, rest = jnp.zeros((1, 88), f32), jnp.zeros((1, 15), f32)
    extra = jnp.concatenate([blank, mask_ref[...], count, rest], axis=1)
    lane = lax.broadcasted_iota(jnp.int32, (1, 128), 1)
    stats = jnp.concatenate([first, jnp.where(lane < 88, last, extra)], axis=0)
    stats_ref[...] = jnp.broadcast_to(stats[None], stats_ref.shape)
    for copy in sent:
        copy.wait()


def logits_of(got, own, far, mass, mask, far_mask):
    wide = pltpu.HBM((192, 1024), f32)
    stats = jax.ShapeDtypeStruct((64, 2, 128), f32)
    return pl.pallas_call(
        logits_kernel,
        in_specs=[IN_VMEM, IN_VMEM, IN_HBM] + [IN_VMEM] * 3,
        out_specs=(IN_HBM, IN_VMEM),
        out_shape=(wide, stats),
        scratch_shapes=[
            pltpu.VMEM(HELD, bf16),
            pltpu.VMEM((4, 192, 256), f32),
            pltpu.SemaphoreType.DMA((2,)),
            pltpu.SemaphoreType.DMA((4,)),
        ],
        compiler_params=KERNEL,
    )(got, own, in_hbm(far), mass, mask, far_mask)


def teacher_kernel(probs_ref, near_ref, give_ref, mass_ref):
    y_at, core = lax.axis_index("yh"), lax.axis_index("c")
    for x_at in range(4):
        for out_ref, y_of in ((near_ref, y_at), (give_ref, 1 - y_at)):
            for which, core_of in enumerate((core, 1 - core)):
                start = pl.multiple_of(2048 * x_at + 1024 * y_of + 512 * core_of, 512)
                out_ref[x_at, :, 512 * which : 512 * which + 512] = probs_ref[:, pl.ds(start, 512)]
    total = probs_ref[:, :128].astype(f32)
    for start in range(128, 8192, 128):
        total = total + probs_ref[:, start : start + 128].astype(f32)
    mass_ref[...] = jnp.broadcast_to(jnp.sum(total, axis=1, keepdims=True), (24, 128))


def teacher_parts(probs):
    part = jax.ShapeDtypeStruct((4, 24, 1024), bf16)
    out = (part, part, jax.ShapeDtypeStruct((24, 128), f32))
    return pl.pallas_call(teacher_kernel, out_shape=out, compiler_params=KERNEL)(probs)


def stats_kernel(stats_ref, target_ref, out_ref):
    first = stats_ref[0, :1, :]
    for at in range(1, 64):
        first = first + stats_ref[at, :1, :]
    halves = []
    for y_at in range(2):
        total = stats_ref[32 * y_at, 1:, :]
        for at in range(1, 32):
            total = total + stats_ref[32 * y_at + at, 1:, :]
        halves.append(total)
    lane = lax.broadcasted_iota(jnp.int32, (1, 128), 1)
    low = jnp.where(lane < 88, halves[0], stats_ref[0, 1:, :])
    high = jnp.where(lane < 88, halves[1], stats_ref[32, 1:, :])
    low = jnp.where(lane < 64, halves[0] + halves[1], low)
    rows = jnp.concatenate([first, low, high, high], axis=0)
    top = rows.astype(bf16).astype(f32)
    middle = (rows - top).astype(bf16).astype(f32)
    split = [top, middle, rows - top - middle, jnp.zeros((36, 128), f32)]
    split = jnp.concatenate(split, axis=0).astype(bf16)
    for at in range(4):
        out_ref[at, :, :1024] = target_ref[at]
        out_ref[at, :, 1024:] = split


def stats_over_plane(stats, target):
    out = jax.ShapeDtypeStruct((4, 48, 1152), bf16)
    return pl.pallas_call(stats_kernel, out_shape=out, compiler_params=KERNEL)(stats, target)


def grads_kernel(
    got_ref,
    tanh_ref,
    own_ref,
    far_ref,
    part_ref,
    grad_own_ref,
    grad_far_ref,
    held,
    made,
    grads,
    sems,
    out_sems,
    grad_sems,
):
    copies = []
    for at in range(6):
        source = (own_ref, far_ref)[at % 2].at[pl.ds(768 * (at // 2), 768), :]
        copies.append(pltpu.make_async_copy(source, held.at[at], sems.at[at]))
        copies[at].start()
    stats = []
    for at in range(4):
        split = got_ref[at, :, 1024:].astype(f32)
        stats.append(split[0:4] + split[4:8] + split[8:12])
    firsts = [stats[at][:1] for at in range(4)]
    seconds = [stats[at // 2][1 + at % 2 : 2 + at % 2] for at in range(8)]
    rows = jnp.concatenate([sum(firsts), sum(seconds[::2])] + seconds, axis=0)
    lane = lax.broadcasted_iota(jnp.int32, (1, 128), 1)
    counted = jnp.where((lane >= 88) & (lane < 113), sum(seconds), 0.0)
    factor = 8.0 * 262144 / jnp.sum(counted, axis=1, keepdims=True)
    columns = jnp.transpose(jnp.concatenate([rows, jnp.zeros((118, 128), f32)], axis=0))
    sum_exp = jnp.concatenate([columns[:, 0:1], columns[:64, 1:2]], axis=0)
    mass = jnp.concatenate([columns[64:88, 2 + at : 3 + at] for at in range(8)], axis=0)
    mask = jnp.concatenate([columns[88:112, 2 + at : 3 + at] for at in range(8)], axis=0)
    scale, share = factor * mask, mass / sum_exp
    sent = []
    for at, grad_ref in enumerate((grad_own_ref, grad_far_ref)):
        entries = slice(512 * at, 512 * at + 512)
        capped_tanh = tanh_ref[:, entries]
        target = jnp.concatenate([got_ref[x_at, :, entries].astype(f32) for x_at in range(4)])
        grad = jnp.exp(30.0 * capped_tanh) * share - target
        grads[at] = (scale * grad * (1.0 - capped_tanh * capped_tanh)).astype(bf16)
        sent.append(pltpu.make_async_copy(grads.at[at], grad_ref, grad_sems.at[at]))
        sent[at].start()
    dims = (((1,), (1,)), ((), ()))
    for at in range(3):
        copies[2 * at].wait()
        copies[2 * at + 1].wait()
        for start in (0, 384):
            inner = slice(start, start + 384)
            part = lax.dot_general(
                grads[0], held[2 * at, inner, :], dims, preferred_element_type=f32
            ) + lax.dot_general(
                grads[1], held[2 * at + 1, inner, :], dims, preferred_element_type=f32
            )
            part = part.astype(bf16)
            for x_at in range(4):
                made[at, x_at, :, inner] = part[48 * x_at : 48 * x_at + 48]
        target = part_ref.at[:, :, pl.ds(768 * at, 768)]
        sent.append(pltpu.make_async_copy(made.at[at], target, out_sems.at[at]))
        sent[2 + at].start()
    for copy in sent:
        copy.wait()


def grads_of(got, capped_tanh, own, far):
    grad = pltpu.HBM((192, 512), bf16)
    return pl.pallas_call(
        grads_kernel,
        in_specs=[IN_VMEM] * 2 + [IN_HBM] * 2,
        out_specs=(IN_HBM, IN_HBM, IN_HBM),
        out_shape=(pltpu.HBM((4, 48, own.shape[0]), bf16), grad, grad),
        scratch_shapes=[
            pltpu.VMEM((6, 768, 512), bf16),
            pltpu.VMEM((3, 4, 48, 768), bf16),
            pltpu.VMEM((2, 192, 512), bf16),
            pltpu.SemaphoreType.DMA((6,)),
            pltpu.SemaphoreType.DMA((3,)),
            pltpu.SemaphoreType.DMA((2,)),
        ],
        compiler_params=KERNEL,
    )(got, capped_tanh, in_hbm(own), in_hbm(far))


def packed(block):
    first, second, third = block[:8], block[8:16], block[16:]
    top = jnp.concatenate([first, second[:, :56]], axis=1)
    rest = jnp.concatenate([second[:, 56:], third, jnp.zeros((8, 40), block.dtype)], axis=1)
    return jnp.concatenate([top, rest], axis=0)


def unpacked(block):
    top, rest = block[..., :8, :], block[..., 8:, :]
    second = jnp.concatenate([top[..., 72:], rest[..., :16]], axis=-1)
    return jnp.concatenate([top[..., :72], second, rest[..., 16:88]], axis=-2)


def pack_copies_kernel(block_ref, out_ref):
    block = packed(block_ref[...].astype(f32)).astype(bf16)
    out_ref[...] = jnp.broadcast_to(block[None], out_ref.shape)


def pack_copies(block):
    out = jax.ShapeDtypeStruct((64, 16, 128), bf16)
    return pl.pallas_call(pack_copies_kernel, out_shape=out, compiler_params=KERNEL)(block)


def sum_pack_kernel(parts_ref, out_ref, held, sems):
    copies = []
    for at in range(2):
        source = parts_ref.at[:, :, pl.ds(1152 * at, 1152)]
        copies.append(pltpu.make_async_copy(source, held.at[at], sems.at[at]))
        copies[at].start()
    for at in range(2):
        copies[at].wait()
        total = held[at, 0].astype(f32)
        for x_at in range(1, 4):
            total = total + held[at, x_at].astype(f32)
        for shard in range(16):
            columns = total[:, 72 * shard : 72 * shard + 72]
            for y_at in range(2):
                block = packed(columns[24 * y_at : 24 * y_at + 24])
                out_ref[32 * y_at + 16 * at + shard] = block.astype(bf16)


def sum_pack(parts):
    return pl.pallas_call(
        sum_pack_kernel,
        in_specs=[IN_HBM],
        out_shape=jax.ShapeDtypeStruct((64, 16, 128), bf16),
        scratch_shapes=[pltpu.VMEM((2, 4, 48, 1152), bf16), pltpu.SemaphoreType.DMA((2,))],
        compiler_params=KERNEL,
    )(parts)


def shards(hidden_states, loss_mask, teacher_probs, head_weight):
    tokens, features = hidden_states.shape
    feature_dim, shard_cols = head_weight.shape[0], head_weight.shape[3]
    half = 8 * tokens
    weight = head_weight.reshape(feature_dim, shard_cols)
    y_at = lax.axis_index("yh")

    copies, weight, teacher_probs, loss_mask = lax.optimization_barrier(
        (pack_copies(hidden_states), weight, teacher_probs, loss_mask)
    )
    plane = unpacked(lax.all_to_all(copies, PLANE, 0, 0, tiled=True))
    plane = plane.reshape(2, 32, tokens, features)
    rows = plane.transpose(0, 2, 1, 3).reshape(2 * tokens, feature_dim)

    weight_other = lax.ppermute(weight, "c", SWAP)
    mask_mine = loss_mask.astype(f32)
    mask_other = lax.ppermute(mask_mine, "c", SWAP)

    near, give, mass_part = teacher_parts(teacher_probs)
    came = lax.ppermute(give, "yh", SWAP)

    rows, mask_other = lax.optimization_barrier((rows, mask_other))
    got = lax.all_gather(rows, "x", axis=0)
    got, came = lax.optimization_barrier((got, came))
    low, high = jnp.where(y_at == 0, near, came), jnp.where(y_at == 0, came, near)
    target = jnp.concatenate([low, high], axis=1)

    capped_tanh, stats = logits_of(
        got, weight, weight_other, mass_part, mask_mine[None], mask_other[None]
    )
    stats = stats_over_plane(lax.all_to_all(stats, PLANE, 0, 0, tiled=True), target)
    stats = lax.all_to_all(stats, "x", 0, 0, tiled=True)
    part, grad_own, grad_far = grads_of(stats, capped_tanh, weight, weight_other)
    mine = got.reshape(half, feature_dim)

    states = jnp.concatenate([mine, lax.ppermute(mine, "c", SWAP)])
    grad_logits = jnp.concatenate([grad_own, lax.ppermute(grad_far, "c", SWAP)])
    head_grad = lax.dot_general(
        states, grad_logits, (((0,), (0,)), ((), ())), preferred_element_type=f32
    )
    grad_head = head_grad.astype(bf16).reshape(head_weight.shape)

    part = sum_pack(lax.all_to_all(part, "x", 0, 0, tiled=True))
    part = lax.all_to_all(part, PLANE, 0, 0, tiled=True)
    grad_hidden = unpacked(jnp.sum(part.astype(f32), axis=0)).astype(bf16)
    return grad_hidden, grad_head


def solution(mesh):
    fine = Mesh(mesh.devices.reshape(tuple(SIZES.values())), tuple(SIZES))
    head = P(None, VOCAB, SEQ, None)
    return jax.shard_map(
        shards,
        mesh=fine,
        in_specs=(P(SEQ, VOCAB), P(SEQ), P(SEQ, VOCAB), head),
        out_specs=(P(SEQ, VOCAB), head),
        check_vma=False,
    )
```

time: 131 us -> 123 us (0.939)
  blocking collectives: 37.2 us -> 24.7 us
  waiting for transfers between devices: 25.5 us -> 30 us
  starting transfers between devices: 44.5 us -> 46.8 us
  Pallas kernels: 13.5 us -> 11.4 us
    all_to_all x2 -> x1, blocking collectives: 37.2 us -> 10.5 us  [shards(): stats = lax.all_to_all(stats, 'x', 0, 0, tiled=True)]
    all_gather x0 -> x1, blocking collectives: none -> 14.2 us  [shards(): got = lax.all_gather(rows, 'x', axis=0)]
    all_to_all x1, waiting for transfers between devices: 3.74 us -> 11.2 us  [shards(): lax.all_to_all(stats, PLANE, 0, 0, tiled=True)]
    all_to_all x1, waiting for transfers between devices: 6.32 us -> 3.28 us  [shards(): plane = unpacked(lax.all_to_all(copies, PLANE, 0, 0, tiled=True))]
    pallas_call x4 -> x5, Pallas kernels: 12.4 us -> 10.3 us  [the longest x1 4.49 us: grads_of(): pl.pallas_call(grads_kernel, in_specs=[IN_VMEM] * 2 + [IN_HBM] * 2, out_s...]
    ppermute x1, starting transfers between devices: 5.29 us -> 7.27 us  [shards(): came = lax.ppermute(give, 'yh', SWAP)]
    unnamed x6 -> x12, local copies, waits for them, and re-layouts: 0.01 us -> 1.69 us
  transfers between devices with their start and end apart: 9 -> 9, of which waited for: 5 -> 5; matrix products, arithmetic and copies ran while one was open for 6% -> 5% of each run, Pallas kernels for 2% -> 2%
where the time goes in v3:
time: 123 us; the launch traced here: 122 us
  starting transfers between devices  46.8 us (38%)
  waiting for transfers between devices  30 us (24%)
  blocking collectives  24.7 us (20%)
  Pallas kernels  11.4 us (9%)
  local copies, waits for them, and re-layouts  3.29 us (3%)
  matrix products  2.83 us (2%)
  other arithmetic  2.53 us (2%)
    all_to_all x1, starting transfers between devices, shards(): plane = unpacked(lax.all_to_all(copies, PLANE, 0, 0, tiled=True))  16.6 us
    all_gather x1, blocking collectives, shards(): got = lax.all_gather(rows, 'x', axis=0)  14.2 us
    all_to_all x1, waiting for transfers between devices, shards(): lax.all_to_all(stats, PLANE, 0, 0, tiled=True)  11.2 us
    all_to_all x1, blocking collectives, shards(): stats = lax.all_to_all(stats, 'x', 0, 0, tiled=True)  10.5 us
    all_to_all x1, waiting for transfers between devices, shards(): part = lax.all_to_all(part, PLANE, 0, 0, tiled=True)  7.49 us
    ppermute x1, starting transfers between devices, shards(): came = lax.ppermute(give, 'yh', SWAP)  7.27 us
    all_to_all x1, waiting for transfers between devices, shards(): part = sum_pack(lax.all_to_all(part, 'x', 0, 0, tiled=True))  6.64 us
    all_to_all x1, starting transfers between devices, shards(): lax.all_to_all(stats, PLANE, 0, 0, tiled=True)  5.29 us
  transfers between devices with their start and end apart: 9, of which 5 were waited for; matrix products, arithmetic and copies ran while one was open for 5% of the time, Pallas kernels for 2%

profile of v3, /device:TPU:2, one launch (start us, length us, event | category | flops | bytes accessed | tf_op | source)
XLA Modules:
  0.0 122.5 jit_solution(15088901796208889833)
XLA Ops:
  0.6 0.0 copy-start.3
  0.6 0.7 copy-done.3
  1.3 0.8 shard_map.59
  2.1 1.9 %collective-permute-start.2 = (bf16[2304,512]{1,0:T(8,128)(2,1)}, bf16[2304,512]{1,0:T(8,128)(2,1)}, u32[]{:S(2)}, u32[]{:S(2)}) collective-permute-start(bf16[2304,512]{1,0:T(8,128)(2,1)} %bitcast.13), channel_id=1, source_target_pairs={{0,32},{32,0},{1,33},{33,1},{2,34},{34,2},{3,35},{35,3},{4,36},{36... | collective-permute-start | bytes 7077896 | tf_op jit(solution)/shard_map/ppermute | solution.py:289
  4.0 16.6 %all-to-all-start = ((bf16[64,16,128]{2,1,0:T(8,128)(2,1)}), bf16[64,16,128]{2,1,0:T(8,128)(2,1)S(1)}, u32[]{:S(2)}, u32[]{:S(2)}) async-start(bf16[64,16,128]{2,1,0:T(8,128)(2,1)} %shard_map.59), calls=%async_computation | async-start | bytes 524288 | tf_op jit(solution)/shard_map/all_to_all | solution.py:285
  20.6 0.7 convert_bitcast_fusion
  21.3 2.2 %collective-permute-start = (f32[24]{0:T(128)S(1)}, f32[24]{0:T(128)S(1)}, u32[]{:S(2)}, u32[]{:S(2)}) collective-permute-start(f32[24]{0:T(128)S(1)} %get-tuple-element.41), channel_id=1, source_target_pairs={{0,32},{32,0},{1,33},{33,1},{2,34},{34,2},{3,35},{35,3},{4,36},{36... | collective-permute-start | bytes 296 | tf_op jit(solution)/shard_map/ppermute | solution.py:291
  23.6 0.0 copy-start.2
  23.6 1.0 copy-done.2
  24.6 0.8 shard_map.60
  25.3 7.3 %collective-permute-start.1 = (bf16[4,24,1024]{2,1,0:T(8,128)(2,1)}, bf16[4,24,1024]{2,1,0:T(8,128)(2,1)}, u32[]{:S(2)}, u32[]{:S(2)}) collective-permute-start(bf16[4,24,1024]{2,1,0:T(8,128)(2,1)} %get-tuple-element.22), channel_id=1, source_target_pairs={{0,64},{64,0},{1,65},{65,1},{2,66},{66,2},{3,67},{67,3},{4,68},{68... | collective-permute-start | bytes 589832 | tf_op jit(solution)/shard_map/ppermute | solution.py:294
  32.6 3.3 %all-to-all-done = bf16[64,16,128]{2,1,0:T(8,128)(2,1)S(1)} async-done(((bf16[64,16,128]{2,1,0:T(8,128)(2,1)}), bf16[64,16,128]{2,1,0:T(8,128)(2,1)S(1)}, u32[]{:S(2)}, u32[]{:S(2)}) %all-to-all-start) | async-done | bytes 262176 | tf_op jit(solution)/shard_map/all_to_all | solution.py:285
  35.9 0.1 slice.49
  36.0 0.1 fusion.8
  36.1 0.1 pad_maximum_fusion
  36.3 0.1 copy.6
  36.3 1.2 reshape.21
  37.5 0.0 collective-permute-done
  37.5 14.2 %all-gather = bf16[192,2304]{1,0:T(8,128)(2,1)S(1)} all-gather(bf16[48,2304]{1,0:T(8,128)(2,1)} %reshape.21), channel_id=2, replica_groups=mesh['x'=4,'yh'=2,'c'=2,'yl'=4,'z'=8] {'x'}, dimensions={0}, use_global_device_ids=true | all-gather | bytes 1105920 | tf_op jit(solution)/shard_map/all_gather | solution.py:297
  51.7 0.0 collective-permute-done.1
  51.7 0.0 collective-permute-done.2.far_ref
  51.7 0.0 copy-done
  51.8 4.2 %shard_map.61 = (f32[192,1024]{1,0:T(8,128)}, f32[64,2,128]{2,1,0:T(2,128)}) custom-call(bf16[4,48,2304]{2,1,0:T(8,128)(2,1)S(1)} %bitcast.16, bf16[2304,512]{1,0:T(8,128)(2,1)S(1)} %bitcast.15, bf16[2304,512]{1,0:T(8,128)(2,1)} %collective-permute-done.2.far_ref, f32[24,128]{1,0:T(8,128)S(1)} %get-tuple-element.25.mass_ref, ...), custom_call_target="tpu_custom_call" | custom-call | tf_op jit(solution)/shard_map/pallas_call | solution.py:77
  56.0 0.0 copy-start.1
  56.0 5.3 %all-to-all-start.1 = ((f32[64,2,128]{2,1,0:T(2,128)}), f32[64,2,128]{2,1,0:T(2,128)S(1)}, u32[]{:S(2)}, u32[]{:S(2)}) async-start(f32[64,2,128]{2,1,0:T(2,128)} %get-tuple-element.27), calls=%async_computation.1 | async-start | bytes 131072 | tf_op jit(solution)/shard_map/all_to_all | solution.py:305
  61.3 1.0 broadcast_select_fusion.1
  62.3 11.2 %all-to-all-done.1.stats_ref = f32[64,2,128]{2,1,0:T(2,128)S(1)} async-done(((f32[64,2,128]{2,1,0:T(2,128)}), f32[64,2,128]{2,1,0:T(2,128)S(1)}, u32[]{:S(2)}, u32[]{:S(2)}) %all-to-all-start.1) | async-done | bytes 65568 | tf_op jit(solution)/shard_map/all_to_all | solution.py:305
  73.4 0.1 shard_map.62
  73.5 10.5 %all_to_all.25.got_ref = bf16[4,48,1152]{2,1,0:T(8,128)(2,1)S(1)} all-to-all(bf16[4,48,1152]{2,1,0:T(8,128)(2,1)S(1)} %shard_map.62), channel_id=1, replica_groups=mesh['x'=4,'yh'=2,'c'=2,'yl'=4,'z'=8] {'x'}, dimensions={0} | all-to-all | bytes 884736 | tf_op jit(solution)/shard_map/all_to_all | solution.py:306
  84.0 0.0 copy-done.1
  84.0 4.5 %shard_map.63 = (bf16[4,48,2304]{2,1,0:T(8,128)(2,1)}, bf16[192,512]{1,0:T(8,128)(2,1)}, bf16[192,512]{1,0:T(8,128)(2,1)}) custom-call(bf16[4,48,1152]{2,1,0:T(8,128)(2,1)S(1)} %all_to_all.25.got_ref, f32[192,1024]{1,0:T(8,128)S(1)} %copy-done.1, bf16[2304,512]{1,0:T(8,128)(2,1)} %bitcast.14, bf16[2304,512]{1,0:T(8,128)(2,1)} %collective-permute-done.2.far_ref), custom_call_target="tpu_custom_call" | custom-call | tf_op jit(solution)/shard_map/pallas_call | solution.py:207
  88.5 0.0 copy-start.5
  88.5 0.0 copy-start.4
  88.5 5.1 %all-to-all-start.3 = ((bf16[4,48,2304]{2,1,0:T(8,128)(2,1)}), bf16[4,48,2304]{2,1,0:T(8,128)(2,1)S(1)}, u32[]{:S(2)}, u32[]{:S(2)}) async-start(bf16[4,48,2304]{2,1,0:T(8,128)(2,1)} %get-tuple-element.31), calls=%async_computation.3 | async-start | bytes 1769472 | tf_op jit(solution)/shard_map/all_to_all | solution.py:317
  93.6 1.9 %collective-permute-start.3 = (bf16[192,2304]{1,0:T(8,128)(2,1)S(1)}, bf16[192,2304]{1,0:T(8,128)(2,1)S(1)}, u32[]{:S(2)}, u32[]{:S(2)}) collective-permute-start(bf16[192,2304]{1,0:T(8,128)(2,1)S(1)} %all-gather), channel_id=1, source_target_pairs={{0,32},{32,0},{1,33},{33,1},{2,34},{34,2},{3,35},{35,3},{4,36},{36... | collective-permute-start | bytes 2654216 | tf_op jit(solution)/shard_map/ppermute | solution.py:310
  95.5 6.6 %all-to-all-done.3.parts_ref = bf16[4,48,2304]{2,1,0:T(8,128)(2,1)S(1)} async-done(((bf16[4,48,2304]{2,1,0:T(8,128)(2,1)}), bf16[4,48,2304]{2,1,0:T(8,128)(2,1)S(1)}, u32[]{:S(2)}, u32[]{:S(2)}) %all-to-all-start.3) | async-done | bytes 884768 | tf_op jit(solution)/shard_map/all_to_all | solution.py:317
  102.2 1.1 shard_map.64
  103.3 4.6 %all-to-all-start.4 = ((bf16[64,16,128]{2,1,0:T(8,128)(2,1)}), bf16[64,16,128]{2,1,0:T(8,128)(2,1)S(1)}, u32[]{:S(2)}, u32[]{:S(2)}) async-start(bf16[64,16,128]{2,1,0:T(8,128)(2,1)} %shard_map.64), calls=%async_computation.4 | async-start | bytes 524288 | tf_op jit(solution)/shard_map/all_to_all | solution.py:318
  107.9 0.0 copy-done.5
  107.9 1.9 %collective-permute-start.4 = (bf16[192,512]{1,0:T(8,128)(2,1)S(1)}, bf16[192,512]{1,0:T(8,128)(2,1)S(1)}, u32[]{:S(2)}, u32[]{:S(2)}) collective-permute-start(bf16[192,512]{1,0:T(8,128)(2,1)S(1)} %copy-done.5), channel_id=1, source_target_pairs={{0,32},{32,0},{1,33},{33,1},{2,34},{34,2},{3,35},{35,3},{4,36},{36... | collective-permute-start | bytes 589832 | tf_op jit(solution)/shard_map/ppermute | solution.py:311
  109.8 0.0 collective-permute-done.3
  109.8 1.4 %collective-permute-done.4 = bf16[192,512]{1,0:T(8,128)(2,1)S(1)} collective-permute-done((bf16[192,512]{1,0:T(8,128)(2,1)S(1)}, bf16[192,512]{1,0:T(8,128)(2,1)S(1)}, u32[]{:S(2)}, u32[]{:S(2)}) %collective-permute-start.4) | collective-permute-done | bytes 196640 | tf_op jit(solution)/shard_map/ppermute | solution.py:311
  111.2 2.8 %fusion = bf16[2304,1,1,512]{3,0,2,1:T(8,128)(2,1)} fusion(bf16[192,2304]{1,0:T(8,128)(2,1)S(1)} %collective-permute-done.3, bf16[192,2304]{1,0:T(8,128)(2,1)S(1)} %all-gather, bf16[192,512]{1,0:T(8,128)(2,1)S(1)} %collective-permute-done.4, bf16[192,512]{1,0:T(8,128)(2,1)S(1)} %copy-done.4), kind=kOutput, calls=%fused_computation.1 | convolution fusion | flops 911474688 | bytes 4521984 | tf_op jit(solution)/shard_map/dot_general | solution.py:312
  114.1 7.5 %all-to-all-done.4 = bf16[64,16,128]{2,1,0:T(8,128)(2,1)S(1)} async-done(((bf16[64,16,128]{2,1,0:T(8,128)(2,1)}), bf16[64,16,128]{2,1,0:T(8,128)(2,1)S(1)}, u32[]{:S(2)}, u32[]{:S(2)}) %all-to-all-start.4) | async-done | bytes 262176 | tf_op jit(solution)/shard_map/all_to_all | solution.py:318
  121.6 0.1 reduce
  121.6 0.1 fusion.9
  121.7 0.1 slice.53
  121.8 0.7 pad_maximum_fusion.2
  (5 shorter events, 0.0 us)
Async XLA Ops:
  0.6 0.7 copy-start.3
  2.1 49.6 %collective-permute-start.2 = (bf16[2304,512]{1,0:T(8,128)(2,1)}, bf16[2304,512]{1,0:T(8,128)(2,1)}, u32[]{:S(2)}, u32[]{:S(2)}) collective-permute-start(bf16[2304,512]{1,0:T(8,128)(2,1)} %bitcast.13), channel_id=1, source_target_pairs={{0,32},{32,0},{1,33},{33,1},{2,34},{34,2},{3,35},{35,3},{4,36},{36... | collective-permute-start | bytes 7077896 | tf_op jit(solution)/shard_map/ppermute | solution.py:289
  4.0 31.9 %all-to-all-start = ((bf16[64,16,128]{2,1,0:T(8,128)(2,1)}), bf16[64,16,128]{2,1,0:T(8,128)(2,1)S(1)}, u32[]{:S(2)}, u32[]{:S(2)}) async-start(bf16[64,16,128]{2,1,0:T(8,128)(2,1)} %shard_map.59), calls=%async_computation | async-start | bytes 524288 | tf_op jit(solution)/shard_map/all_to_all | solution.py:285
  21.3 30.4 %copy-start = (bf16[2304,1,1,512]{3,0,2,1:T(8,128)(2,1)S(1)}, bf16[2304,1,1,512]{3,0,2,1:T(8,128)(2,1)}, u32[]{:S(2)}) copy-start(bf16[2304,1,1,512]{3,0,2,1:T(8,128)(2,1)} %param.7) | copy-start | bytes 7077892
  21.3 16.2 %collective-permute-start = (f32[24]{0:T(128)S(1)}, f32[24]{0:T(128)S(1)}, u32[]{:S(2)}, u32[]{:S(2)}) collective-permute-start(f32[24]{0:T(128)S(1)} %get-tuple-element.41), channel_id=1, source_target_pairs={{0,32},{32,0},{1,33},{33,1},{2,34},{34,2},{3,35},{35,3},{4,36},{36... | collective-permute-start | bytes 296 | tf_op jit(solution)/shard_map/ppermute | solution.py:291
  23.6 1.0 copy-start.2
  25.3 26.4 %collective-permute-start.1 = (bf16[4,24,1024]{2,1,0:T(8,128)(2,1)}, bf16[4,24,1024]{2,1,0:T(8,128)(2,1)}, u32[]{:S(2)}, u32[]{:S(2)}) collective-permute-start(bf16[4,24,1024]{2,1,0:T(8,128)(2,1)} %get-tuple-element.22), channel_id=1, source_target_pairs={{0,64},{64,0},{1,65},{65,1},{2,66},{66,2},{3,67},{67,3},{4,68},{68... | collective-permute-start | bytes 589832 | tf_op jit(solution)/shard_map/ppermute | solution.py:294
  56.0 28.1 %copy-start.1 = (f32[192,1024]{1,0:T(8,128)S(1)}, f32[192,1024]{1,0:T(8,128)}, u32[]{:S(2)}) copy-start(f32[192,1024]{1,0:T(8,128)} %get-tuple-element.30.tanh_ref) | copy-start | bytes 2359300
  56.0 17.4 %all-to-all-start.1 = ((f32[64,2,128]{2,1,0:T(2,128)}), f32[64,2,128]{2,1,0:T(2,128)S(1)}, u32[]{:S(2)}, u32[]{:S(2)}) async-start(f32[64,2,128]{2,1,0:T(2,128)} %get-tuple-element.27), calls=%async_computation.1 | async-start | bytes 131072 | tf_op jit(solution)/shard_map/all_to_all | solution.py:305
  88.5 19.4 %copy-start.5 = (bf16[192,512]{1,0:T(8,128)(2,1)S(1)}, bf16[192,512]{1,0:T(8,128)(2,1)}, u32[]{:S(2)}) copy-start(bf16[192,512]{1,0:T(8,128)(2,1)} %get-tuple-element.33) | copy-start | bytes 589828
  88.5 22.7 %copy-start.4 = (bf16[192,512]{1,0:T(8,128)(2,1)S(1)}, bf16[192,512]{1,0:T(8,128)(2,1)}, u32[]{:S(2)}) copy-start(bf16[192,512]{1,0:T(8,128)(2,1)} %get-tuple-element.32) | copy-start | bytes 589828
  88.5 13.6 %all-to-all-start.3 = ((bf16[4,48,2304]{2,1,0:T(8,128)(2,1)}), bf16[4,48,2304]{2,1,0:T(8,128)(2,1)S(1)}, u32[]{:S(2)}, u32[]{:S(2)}) async-start(bf16[4,48,2304]{2,1,0:T(8,128)(2,1)} %get-tuple-element.31), calls=%async_computation.3 | async-start | bytes 1769472 | tf_op jit(solution)/shard_map/all_to_all | solution.py:317
  93.6 16.2 %collective-permute-start.3 = (bf16[192,2304]{1,0:T(8,128)(2,1)S(1)}, bf16[192,2304]{1,0:T(8,128)(2,1)S(1)}, u32[]{:S(2)}, u32[]{:S(2)}) collective-permute-start(bf16[192,2304]{1,0:T(8,128)(2,1)S(1)} %all-gather), channel_id=1, source_target_pairs={{0,32},{32,0},{1,33},{33,1},{2,34},{34,2},{3,35},{35,3},{4,36},{36... | collective-permute-start | bytes 2654216 | tf_op jit(solution)/shard_map/ppermute | solution.py:310
  103.3 18.3 %all-to-all-start.4 = ((bf16[64,16,128]{2,1,0:T(8,128)(2,1)}), bf16[64,16,128]{2,1,0:T(8,128)(2,1)S(1)}, u32[]{:S(2)}, u32[]{:S(2)}) async-start(bf16[64,16,128]{2,1,0:T(8,128)(2,1)} %shard_map.64), calls=%async_computation.4 | async-start | bytes 524288 | tf_op jit(solution)/shard_map/all_to_all | solution.py:318
  107.9 3.3 %collective-permute-start.4 = (bf16[192,512]{1,0:T(8,128)(2,1)S(1)}, bf16[192,512]{1,0:T(8,128)(2,1)S(1)}, u32[]{:S(2)}, u32[]{:S(2)}) collective-permute-start(bf16[192,512]{1,0:T(8,128)(2,1)S(1)} %copy-done.5), channel_id=1, source_target_pairs={{0,32},{32,0},{1,33},{33,1},{2,34},{34,2},{3,35},{35,3},{4,36},{36... | collective-permute-start | bytes 589832 | tf_op jit(solution)/shard_map/ppermute | solution.py:311

commit v4 on v3

--- a/solution.py
+++ b/solution.py
@@ -61,9 +61,9 @@
     first = jnp.transpose(wide[:128])[:1]
     last = jnp.concatenate([wide[128:], mass_ref[...], jnp.zeros((40, 128), f32)], axis=0)
     last = jnp.transpose(last)[:1]
-    count = jnp.sum(far_mask_ref[...], axis=1, keepdims=True)
+    count = jnp.sum(far_mask_ref[...].astype(f32), axis=1, keepdims=True)
     blank, rest = jnp.zeros((1, 88), f32), jnp.zeros((1, 15), f32)
-    extra = jnp.concatenate([blank, mask_ref[...], count, rest], axis=1)
+    extra = jnp.concatenate([blank, mask_ref[...].astype(f32), count, rest], axis=1)
     lane = lax.broadcasted_iota(jnp.int32, (1, 128), 1)
     stats = jnp.concatenate([first, jnp.where(lane < 88, last, extra)], axis=0)
     stats_ref[...] = jnp.broadcast_to(stats[None], stats_ref.shape)
@@ -241,7 +241,22 @@
 
 def pack_copies(block):
     out = jax.ShapeDtypeStruct((64, 16, 128), bf16)
-    return pl.pallas_call(pack_copies_kernel, out_shape=out, compiler_params=KERNEL)(block)
+    return pl.pallas_call(pack_copies_kernel, out_shape=out)(block)
+
+
+def unpack_rows_kernel(plane_ref, out_ref):
+    rows = [
+        jnp.concatenate(
+            [unpacked(plane_ref[32 * y_at + shard].astype(f32)) for shard in range(32)], axis=1
+        )
+        for y_at in range(2)
+    ]
+    out_ref[...] = jnp.concatenate(rows, axis=0).astype(bf16)
+
+
+def unpack_rows(plane):
+    out = jax.ShapeDtypeStruct((48, 2304), bf16)
+    return pl.pallas_call(unpack_rows_kernel, out_shape=out, compiler_params=KERNEL)(plane)
 
 
 def sum_pack_kernel(parts_ref, out_ref, held, sems):
@@ -282,13 +297,10 @@
     copies, weight, teacher_probs, loss_mask = lax.optimization_barrier(
         (pack_copies(hidden_states), weight, teacher_probs, loss_mask)
     )
-    plane = unpacked(lax.all_to_all(copies, PLANE, 0, 0, tiled=True))
-    plane = plane.reshape(2, 32, tokens, features)
-    rows = plane.transpose(0, 2, 1, 3).reshape(2 * tokens, feature_dim)
+    rows = unpack_rows(lax.all_to_all(copies, PLANE, 0, 0, tiled=True))
 
     weight_other = lax.ppermute(weight, "c", SWAP)
-    mask_mine = loss_mask.astype(f32)
-    mask_other = lax.ppermute(mask_mine, "c", SWAP)
+    mask_other = lax.ppermute(loss_mask, "c", SWAP)
 
     near, give, mass_part = teacher_parts(teacher_probs)
     came = lax.ppermute(give, "yh", SWAP)
@@ -300,7 +312,7 @@
     target = jnp.concatenate([low, high], axis=1)
 
     capped_tanh, stats = logits_of(
-        got, weight, weight_other, mass_part, mask_mine[None], mask_other[None]
+        got, weight, weight_other, mass_part, loss_mask[None], mask_other[None]
     )
     stats = stats_over_plane(lax.all_to_all(stats, PLANE, 0, 0, tiled=True), target)
     stats = lax.all_to_all(stats, "x", 0, 0, tiled=True)

time: 123 us -> 122 us (level)
  local copies, waits for them, and re-layouts: 3.29 us -> 1.81 us
  transfers between devices with their start and end apart: 9 -> 9, of which waited for: 5 -> 5; matrix products, arithmetic and copies ran while one was open for 5% -> 3% of each run, Pallas kernels for 2% -> 2%
where the time goes in v4:
time: 122 us
  starting transfers between devices  46.6 us (38%)
  waiting for transfers between devices  30.9 us (25%)
  blocking collectives  24.5 us (20%)
  Pallas kernels  12.6 us (10%)
  matrix products  2.83 us (2%)
  local copies, waits for them, and re-layouts  1.81 us (1%)
  other arithmetic  1.73 us (1%)
    all_to_all x1, starting transfers between devices, shards(): rows = unpack_rows(lax.all_to_all(copies, PLANE, 0, 0, tiled=True))  16.6 us
    all_gather x1, blocking collectives, shards(): got = lax.all_gather(rows, 'x', axis=0)  14.1 us
    all_to_all x1, waiting for transfers between devices, shards(): lax.all_to_all(stats, PLANE, 0, 0, tiled=True)  11.3 us
    all_to_all x1, blocking collectives, shards(): stats = lax.all_to_all(stats, 'x', 0, 0, tiled=True)  10.4 us
    all_to_all x1, waiting for transfers between devices, shards(): part = lax.all_to_all(part, PLANE, 0, 0, tiled=True)  7.49 us
    ppermute x1, starting transfers between devices, shards(): came = lax.ppermute(give, 'yh', SWAP)  7.27 us
    all_to_all x1, waiting for transfers between devices, shards(): part = sum_pack(lax.all_to_all(part, 'x', 0, 0, tiled=True))  6.64 us
    all_to_all x1, starting transfers between devices, shards(): lax.all_to_all(stats, PLANE, 0, 0, tiled=True)  5.18 us
  transfers between devices with their start and end apart: 9, of which 5 were waited for; matrix products, arithmetic and copies ran while one was open for 3% of the time, Pallas kernels for 2%

profile of v4, /device:TPU:2, one launch (start us, length us, event | category | flops | bytes accessed | tf_op | source)
XLA Modules:
  0.0 121.7 jit_solution(1324003532006472314)
XLA Ops:
  0.6 0.0 copy-start
  0.6 1.6 %shard_map.59 = bf16[64,16,128]{2,1,0:T(8,128)(2,1)} custom-call(bf16[24,72]{1,0:T(8,128)(2,1)} %block_ref.1), custom_call_target="tpu_custom_call" | custom-call | tf_op jit(solution)/shard_map/pallas_call | solution.py:244
  2.3 1.9 %collective-permute-start.2 = (bf16[2304,512]{1,0:T(8,128)(2,1)}, bf16[2304,512]{1,0:T(8,128)(2,1)}, u32[]{:S(2)}, u32[]{:S(2)}) collective-permute-start(bf16[2304,512]{1,0:T(8,128)(2,1)} %bitcast.7), channel_id=1, source_target_pairs={{0,32},{32,0},{1,33},{33,1},{2,34},{34,2},{3,35},{35,3},{4,36},{36... | collective-permute-start | bytes 7077896 | tf_op jit(solution)/shard_map/ppermute | solution.py:302
  4.2 16.6 %all-to-all-start = ((bf16[64,16,128]{2,1,0:T(8,128)(2,1)}), bf16[64,16,128]{2,1,0:T(8,128)(2,1)S(1)}, u32[]{:S(2)}, u32[]{:S(2)}) async-start(bf16[64,16,128]{2,1,0:T(8,128)(2,1)} %shard_map.59), calls=%async_computation | async-start | bytes 524288 | tf_op jit(solution)/shard_map/all_to_all | solution.py:300
  20.8 2.1 %collective-permute-start = (s32[24]{0:T(128)}, s32[24]{0:T(128)S(1)}, u32[]{:S(2)}, u32[]{:S(2)}) collective-permute-start(s32[24]{0:T(128)} %param.5), channel_id=1, source_target_pairs={{0,32},{32,0},{1,33},{33,1},{2,34},{34,2},{3,35},{35,3},{4,36},{36... | collective-permute-start | bytes 296 | tf_op jit(solution)/shard_map/ppermute | solution.py:303
  22.9 0.0 copy-start.2
  23.0 1.0 copy-done.2
  23.9 0.8 shard_map.61
  24.7 7.3 %collective-permute-start.1 = (bf16[4,24,1024]{2,1,0:T(8,128)(2,1)}, bf16[4,24,1024]{2,1,0:T(8,128)(2,1)}, u32[]{:S(2)}, u32[]{:S(2)}) collective-permute-start(bf16[4,24,1024]{2,1,0:T(8,128)(2,1)} %get-tuple-element.22), channel_id=1, source_target_pairs={{0,64},{64,0},{1,65},{65,1},{2,66},{66,2},{3,67},{67,3},{4,68},{68... | collective-permute-start | bytes 589832 | tf_op jit(solution)/shard_map/ppermute | solution.py:306
  32.0 4.1 %all-to-all-done.plane_ref = bf16[64,16,128]{2,1,0:T(8,128)(2,1)S(1)} async-done(((bf16[64,16,128]{2,1,0:T(8,128)(2,1)}), bf16[64,16,128]{2,1,0:T(8,128)(2,1)S(1)}, u32[]{:S(2)}, u32[]{:S(2)}) %all-to-all-start) | async-done | bytes 262176 | tf_op jit(solution)/shard_map/all_to_all | solution.py:300
  36.1 0.3 shard_map.60
  36.4 0.0 collective-permute-done
  36.4 14.1 %all-gather = bf16[192,2304]{1,0:T(8,128)(2,1)S(1)} all-gather(bf16[48,2304]{1,0:T(8,128)(2,1)S(1)} %shard_map.60), channel_id=2, replica_groups=mesh['x'=4,'yh'=2,'c'=2,'yl'=4,'z'=8] {'x'}, dimensions={0}, use_global_device_ids=true | all-gather | bytes 1105920 | tf_op jit(solution)/shard_map/all_gather | solution.py:309
  50.5 0.0 collective-permute-done.1
  50.5 0.0 collective-permute-done.2.far_ref
  50.5 0.0 copy-done
  50.5 0.0 copy-start.3
  50.5 0.6 copy-done.3
  51.2 4.2 %shard_map.62 = (f32[192,1024]{1,0:T(8,128)}, f32[64,2,128]{2,1,0:T(2,128)}) custom-call(bf16[4,48,2304]{2,1,0:T(8,128)(2,1)S(1)} %bitcast.10, bf16[2304,512]{1,0:T(8,128)(2,1)S(1)} %bitcast.9, bf16[2304,512]{1,0:T(8,128)(2,1)} %collective-permute-done.2.far_ref, f32[24,128]{1,0:T(8,128)S(1)} %get-tuple-element.25.mass_ref, s32[1,24]{1,0:T(1,128)S(1)} %bitcast.11, ...), custom_call_target="tpu_custom_call" | custom-call | tf_op jit(solution)/shard_map/pallas_call | solution.py:77
  55.3 0.0 copy-start.1
  55.4 5.2 %all-to-all-start.1 = ((f32[64,2,128]{2,1,0:T(2,128)}), f32[64,2,128]{2,1,0:T(2,128)S(1)}, u32[]{:S(2)}, u32[]{:S(2)}) async-start(f32[64,2,128]{2,1,0:T(2,128)} %get-tuple-element.27), calls=%async_computation.1 | async-start | bytes 131072 | tf_op jit(solution)/shard_map/all_to_all | solution.py:317
  60.6 1.0 broadcast_select_fusion.1
  61.6 11.3 %all-to-all-done.1.stats_ref = f32[64,2,128]{2,1,0:T(2,128)S(1)} async-done(((f32[64,2,128]{2,1,0:T(2,128)}), f32[64,2,128]{2,1,0:T(2,128)S(1)}, u32[]{:S(2)}, u32[]{:S(2)}) %all-to-all-start.1) | async-done | bytes 65568 | tf_op jit(solution)/shard_map/all_to_all | solution.py:317
  72.8 0.1 shard_map.63
  72.9 10.4 %all_to_all.25.got_ref = bf16[4,48,1152]{2,1,0:T(8,128)(2,1)S(1)} all-to-all(bf16[4,48,1152]{2,1,0:T(8,128)(2,1)S(1)} %shard_map.63), channel_id=1, replica_groups=mesh['x'=4,'yh'=2,'c'=2,'yl'=4,'z'=8] {'x'}, dimensions={0} | all-to-all | bytes 884736 | tf_op jit(solution)/shard_map/all_to_all | solution.py:318
  83.3 0.0 copy-done.1
  83.3 4.5 %shard_map.64 = (bf16[4,48,2304]{2,1,0:T(8,128)(2,1)}, bf16[192,512]{1,0:T(8,128)(2,1)}, bf16[192,512]{1,0:T(8,128)(2,1)}) custom-call(bf16[4,48,1152]{2,1,0:T(8,128)(2,1)S(1)} %all_to_all.25.got_ref, f32[192,1024]{1,0:T(8,128)S(1)} %copy-done.1, bf16[2304,512]{1,0:T(8,128)(2,1)} %bitcast.8, bf16[2304,512]{1,0:T(8,128)(2,1)} %collective-permute-done.2.far_ref), custom_call_target="tpu_custom_call" | custom-call | tf_op jit(solution)/shard_map/pallas_call | solution.py:207
  87.8 0.0 copy-start.5
  87.8 0.0 copy-start.4
  87.8 5.1 %all-to-all-start.3 = ((bf16[4,48,2304]{2,1,0:T(8,128)(2,1)}), bf16[4,48,2304]{2,1,0:T(8,128)(2,1)S(1)}, u32[]{:S(2)}, u32[]{:S(2)}) async-start(bf16[4,48,2304]{2,1,0:T(8,128)(2,1)} %get-tuple-element.31), calls=%async_computation.3 | async-start | bytes 1769472 | tf_op jit(solution)/shard_map/all_to_all | solution.py:329
  92.9 1.9 %collective-permute-start.3 = (bf16[192,2304]{1,0:T(8,128)(2,1)S(1)}, bf16[192,2304]{1,0:T(8,128)(2,1)S(1)}, u32[]{:S(2)}, u32[]{:S(2)}) collective-permute-start(bf16[192,2304]{1,0:T(8,128)(2,1)S(1)} %all-gather), channel_id=1, source_target_pairs={{0,32},{32,0},{1,33},{33,1},{2,34},{34,2},{3,35},{35,3},{4,36},{36... | collective-permute-start | bytes 2654216 | tf_op jit(solution)/shard_map/ppermute | solution.py:322
  94.8 6.6 %all-to-all-done.3.parts_ref = bf16[4,48,2304]{2,1,0:T(8,128)(2,1)S(1)} async-done(((bf16[4,48,2304]{2,1,0:T(8,128)(2,1)}), bf16[4,48,2304]{2,1,0:T(8,128)(2,1)S(1)}, u32[]{:S(2)}, u32[]{:S(2)}) %all-to-all-start.3) | async-done | bytes 884768 | tf_op jit(solution)/shard_map/all_to_all | solution.py:329
  101.4 1.1 shard_map.65
  102.5 4.6 %all-to-all-start.4 = ((bf16[64,16,128]{2,1,0:T(8,128)(2,1)}), bf16[64,16,128]{2,1,0:T(8,128)(2,1)S(1)}, u32[]{:S(2)}, u32[]{:S(2)}) async-start(bf16[64,16,128]{2,1,0:T(8,128)(2,1)} %shard_map.65), calls=%async_computation.4 | async-start | bytes 524288 | tf_op jit(solution)/shard_map/all_to_all | solution.py:330
  107.2 0.0 copy-done.5
  107.2 1.9 %collective-permute-start.4 = (bf16[192,512]{1,0:T(8,128)(2,1)S(1)}, bf16[192,512]{1,0:T(8,128)(2,1)S(1)}, u32[]{:S(2)}, u32[]{:S(2)}) collective-permute-start(bf16[192,512]{1,0:T(8,128)(2,1)S(1)} %copy-done.5), channel_id=1, source_target_pairs={{0,32},{32,0},{1,33},{33,1},{2,34},{34,2},{3,35},{35,3},{4,36},{36... | collective-permute-start | bytes 589832 | tf_op jit(solution)/shard_map/ppermute | solution.py:323
  109.1 0.0 collective-permute-done.3
  109.1 1.4 %collective-permute-done.4 = bf16[192,512]{1,0:T(8,128)(2,1)S(1)} collective-permute-done((bf16[192,512]{1,0:T(8,128)(2,1)S(1)}, bf16[192,512]{1,0:T(8,128)(2,1)S(1)}, u32[]{:S(2)}, u32[]{:S(2)}) %collective-permute-start.4) | collective-permute-done | bytes 196640 | tf_op jit(solution)/shard_map/ppermute | solution.py:323
  110.5 0.0 copy-done.4
  110.5 2.8 %fusion = bf16[2304,1,1,512]{3,0,2,1:T(8,128)(2,1)} fusion(bf16[192,2304]{1,0:T(8,128)(2,1)S(1)} %collective-permute-done.3, bf16[192,2304]{1,0:T(8,128)(2,1)S(1)} %all-gather, bf16[192,512]{1,0:T(8,128)(2,1)S(1)} %collective-permute-done.4, bf16[192,512]{1,0:T(8,128)(2,1)S(1)} %copy-done.4), kind=kOutput, calls=%fused_computation.1 | convolution fusion | flops 911474688 | bytes 4521984 | tf_op jit(solution)/shard_map/dot_general | solution.py:324
  113.3 7.5 %all-to-all-done.4 = bf16[64,16,128]{2,1,0:T(8,128)(2,1)S(1)} async-done(((bf16[64,16,128]{2,1,0:T(8,128)(2,1)}), bf16[64,16,128]{2,1,0:T(8,128)(2,1)S(1)}, u32[]{:S(2)}, u32[]{:S(2)}) %all-to-all-start.4) | async-done | bytes 262176 | tf_op jit(solution)/shard_map/all_to_all | solution.py:330
  120.8 0.1 reduce
  120.9 0.1 fusion.8
  121.0 0.1 slice.27
  121.0 0.7 pad_maximum_fusion.1
  (2 shorter events, 0.0 us)
Async XLA Ops:
  0.6 49.9 %copy-start = (bf16[2304,1,1,512]{3,0,2,1:T(8,128)(2,1)S(1)}, bf16[2304,1,1,512]{3,0,2,1:T(8,128)(2,1)}, u32[]{:S(2)}) copy-start(bf16[2304,1,1,512]{3,0,2,1:T(8,128)(2,1)} %param.7) | copy-start | bytes 7077892
  2.3 48.2 %collective-permute-start.2 = (bf16[2304,512]{1,0:T(8,128)(2,1)}, bf16[2304,512]{1,0:T(8,128)(2,1)}, u32[]{:S(2)}, u32[]{:S(2)}) collective-permute-start(bf16[2304,512]{1,0:T(8,128)(2,1)} %bitcast.7), channel_id=1, source_target_pairs={{0,32},{32,0},{1,33},{33,1},{2,34},{34,2},{3,35},{35,3},{4,36},{36... | collective-permute-start | bytes 7077896 | tf_op jit(solution)/shard_map/ppermute | solution.py:302
  4.2 31.9 %all-to-all-start = ((bf16[64,16,128]{2,1,0:T(8,128)(2,1)}), bf16[64,16,128]{2,1,0:T(8,128)(2,1)S(1)}, u32[]{:S(2)}, u32[]{:S(2)}) async-start(bf16[64,16,128]{2,1,0:T(8,128)(2,1)} %shard_map.59), calls=%async_computation | async-start | bytes 524288 | tf_op jit(solution)/shard_map/all_to_all | solution.py:300
  20.8 15.6 %collective-permute-start = (s32[24]{0:T(128)}, s32[24]{0:T(128)S(1)}, u32[]{:S(2)}, u32[]{:S(2)}) collective-permute-start(s32[24]{0:T(128)} %param.5), channel_id=1, source_target_pairs={{0,32},{32,0},{1,33},{33,1},{2,34},{34,2},{3,35},{35,3},{4,36},{36... | collective-permute-start | bytes 296 | tf_op jit(solution)/shard_map/ppermute | solution.py:303
  22.9 1.0 copy-start.2
  24.7 25.8 %collective-permute-start.1 = (bf16[4,24,1024]{2,1,0:T(8,128)(2,1)}, bf16[4,24,1024]{2,1,0:T(8,128)(2,1)}, u32[]{:S(2)}, u32[]{:S(2)}) collective-permute-start(bf16[4,24,1024]{2,1,0:T(8,128)(2,1)} %get-tuple-element.22), channel_id=1, source_target_pairs={{0,64},{64,0},{1,65},{65,1},{2,66},{66,2},{3,67},{67,3},{4,68},{68... | collective-permute-start | bytes 589832 | tf_op jit(solution)/shard_map/ppermute | solution.py:306
  50.5 0.7 copy-start.3
  55.3 27.9 %copy-start.1 = (f32[192,1024]{1,0:T(8,128)S(1)}, f32[192,1024]{1,0:T(8,128)}, u32[]{:S(2)}) copy-start(f32[192,1024]{1,0:T(8,128)} %get-tuple-element.30.tanh_ref) | copy-start | bytes 2359300
  55.4 17.5 %all-to-all-start.1 = ((f32[64,2,128]{2,1,0:T(2,128)}), f32[64,2,128]{2,1,0:T(2,128)S(1)}, u32[]{:S(2)}, u32[]{:S(2)}) async-start(f32[64,2,128]{2,1,0:T(2,128)} %get-tuple-element.27), calls=%async_computation.1 | async-start | bytes 131072 | tf_op jit(solution)/shard_map/all_to_all | solution.py:317
  87.8 19.4 %copy-start.5 = (bf16[192,512]{1,0:T(8,128)(2,1)S(1)}, bf16[192,512]{1,0:T(8,128)(2,1)}, u32[]{:S(2)}) copy-start(bf16[192,512]{1,0:T(8,128)(2,1)} %get-tuple-element.33) | copy-start | bytes 589828
  87.8 22.7 %copy-start.4 = (bf16[192,512]{1,0:T(8,128)(2,1)S(1)}, bf16[192,512]{1,0:T(8,128)(2,1)}, u32[]{:S(2)}) copy-start(bf16[192,512]{1,0:T(8,128)(2,1)} %get-tuple-element.32) | copy-start | bytes 589828
  87.8 13.6 %all-to-all-start.3 = ((bf16[4,48,2304]{2,1,0:T(8,128)(2,1)}), bf16[4,48,2304]{2,1,0:T(8,128)(2,1)S(1)}, u32[]{:S(2)}, u32[]{:S(2)}) async-start(bf16[4,48,2304]{2,1,0:T(8,128)(2,1)} %get-tuple-element.31), calls=%async_computation.3 | async-start | bytes 1769472 | tf_op jit(solution)/shard_map/all_to_all | solution.py:329
  92.9 16.2 %collective-permute-start.3 = (bf16[192,2304]{1,0:T(8,128)(2,1)S(1)}, bf16[192,2304]{1,0:T(8,128)(2,1)S(1)}, u32[]{:S(2)}, u32[]{:S(2)}) collective-permute-start(bf16[192,2304]{1,0:T(8,128)(2,1)S(1)} %all-gather), channel_id=1, source_target_pairs={{0,32},{32,0},{1,33},{33,1},{2,34},{34,2},{3,35},{35,3},{4,36},{36... | collective-permute-start | bytes 2654216 | tf_op jit(solution)/shard_map/ppermute | solution.py:322
  102.5 18.3 %all-to-all-start.4 = ((bf16[64,16,128]{2,1,0:T(8,128)(2,1)}), bf16[64,16,128]{2,1,0:T(8,128)(2,1)S(1)}, u32[]{:S(2)}, u32[]{:S(2)}) async-start(bf16[64,16,128]{2,1,0:T(8,128)(2,1)} %shard_map.65), calls=%async_computation.4 | async-start | bytes 524288 | tf_op jit(solution)/shard_map/all_to_all | solution.py:330
  107.2 3.3 %collective-permute-start.4 = (bf16[192,512]{1,0:T(8,128)(2,1)S(1)}, bf16[192,512]{1,0:T(8,128)(2,1)S(1)}, u32[]{:S(2)}, u32[]{:S(2)}) collective-permute-start(bf16[192,512]{1,0:T(8,128)(2,1)S(1)} %copy-done.5), channel_id=1, source_target_pairs={{0,32},{32,0},{1,33},{33,1},{2,34},{34,2},{3,35},{35,3},{4,36},{36... | collective-permute-start | bytes 589832 | tf_op jit(solution)/shard_map/ppermute | solution.py:323

commit v5 on v4

--- a/solution.py
+++ b/solution.py
@@ -259,6 +259,21 @@
     return pl.pallas_call(unpack_rows_kernel, out_shape=out, compiler_params=KERNEL)(plane)
 
 
+def sum_unpack_kernel(parts_ref, out_ref):
+    totals = []
+    for start in range(0, 64, 16):
+        total = parts_ref[start].astype(f32)
+        for at in range(start + 1, start + 16):
+            total = total + parts_ref[at].astype(f32)
+        totals.append(total)
+    out_ref[...] = unpacked(sum(totals)).astype(bf16)
+
+
+def sum_unpack(parts):
+    out = jax.ShapeDtypeStruct((24, 72), bf16)
+    return pl.pallas_call(sum_unpack_kernel, out_shape=out, compiler_params=KERNEL)(parts)
+
+
 def sum_pack_kernel(parts_ref, out_ref, held, sems):
     copies = []
     for at in range(2):
@@ -327,8 +342,7 @@
     grad_head = head_grad.astype(bf16).reshape(head_weight.shape)
 
     part = sum_pack(lax.all_to_all(part, "x", 0, 0, tiled=True))
-    part = lax.all_to_all(part, PLANE, 0, 0, tiled=True)
-    grad_hidden = unpacked(jnp.sum(part.astype(f32), axis=0)).astype(bf16)
+    grad_hidden = sum_unpack(lax.all_to_all(part, PLANE, 0, 0, tiled=True))
     return grad_hidden, grad_head
 
 

time: 122 us -> 122 us (level)
  no operation moved by 1% of the time
where the time goes in v5:
time: 122 us
  starting transfers between devices  46.6 us (38%)
  waiting for transfers between devices  30.8 us (25%)
  blocking collectives  24.7 us (20%)
  Pallas kernels  13.3 us (11%)
  matrix products  2.83 us (2%)
  local copies, waits for them, and re-layouts  1.66 us (1%)
    all_to_all x1, starting transfers between devices, shards(): rows = unpack_rows(lax.all_to_all(copies, PLANE, 0, 0, tiled=True))  16.6 us
    all_gather x1, blocking collectives, shards(): got = lax.all_gather(rows, 'x', axis=0)  14.1 us
    all_to_all x1, waiting for transfers between devices, shards(): lax.all_to_all(stats, PLANE, 0, 0, tiled=True)  11.2 us
    all_to_all x1, blocking collectives, shards(): stats = lax.all_to_all(stats, 'x', 0, 0, tiled=True)  10.6 us
    all_to_all x1, waiting for transfers between devices, shards(): grad_hidden = sum_unpack(lax.all_to_all(part, PLANE, 0, 0, tiled=True))  7.49 us
    ppermute x1, starting transfers between devices, shards(): came = lax.ppermute(give, 'yh', SWAP)  7.27 us
    all_to_all x1, waiting for transfers between devices, shards(): part = sum_pack(lax.all_to_all(part, 'x', 0, 0, tiled=True))  6.64 us
    all_to_all x1, starting transfers between devices, shards(): lax.all_to_all(stats, PLANE, 0, 0, tiled=True)  5.18 us
  transfers between devices with their start and end apart: 9, of which 5 were waited for; matrix products, arithmetic and copies ran while one was open for 3% of the time, Pallas kernels for 2%

profile of v5, /device:TPU:2, one launch (start us, length us, event | category | flops | bytes accessed | tf_op | source)
XLA Modules:
  0.0 121.7 jit_solution(971937684254673697)
XLA Ops:
  0.6 0.0 copy-start
  0.6 1.6 %shard_map.59 = bf16[64,16,128]{2,1,0:T(8,128)(2,1)} custom-call(bf16[24,72]{1,0:T(8,128)(2,1)} %block_ref.1), custom_call_target="tpu_custom_call" | custom-call | tf_op jit(solution)/shard_map/pallas_call | solution.py:244
  2.3 1.9 %collective-permute-start.2 = (bf16[2304,512]{1,0:T(8,128)(2,1)}, bf16[2304,512]{1,0:T(8,128)(2,1)}, u32[]{:S(2)}, u32[]{:S(2)}) collective-permute-start(bf16[2304,512]{1,0:T(8,128)(2,1)} %bitcast.7), channel_id=1, source_target_pairs={{0,32},{32,0},{1,33},{33,1},{2,34},{34,2},{3,35},{35,3},{4,36},{36... | collective-permute-start | bytes 7077896 | tf_op jit(solution)/shard_map/ppermute | solution.py:317
  4.2 16.6 %all-to-all-start = ((bf16[64,16,128]{2,1,0:T(8,128)(2,1)}), bf16[64,16,128]{2,1,0:T(8,128)(2,1)S(1)}, u32[]{:S(2)}, u32[]{:S(2)}) async-start(bf16[64,16,128]{2,1,0:T(8,128)(2,1)} %shard_map.59), calls=%async_computation | async-start | bytes 524288 | tf_op jit(solution)/shard_map/all_to_all | solution.py:315
  20.8 2.1 %collective-permute-start = (s32[24]{0:T(128)}, s32[24]{0:T(128)S(1)}, u32[]{:S(2)}, u32[]{:S(2)}) collective-permute-start(s32[24]{0:T(128)} %param.5), channel_id=1, source_target_pairs={{0,32},{32,0},{1,33},{33,1},{2,34},{34,2},{3,35},{35,3},{4,36},{36... | collective-permute-start | bytes 296 | tf_op jit(solution)/shard_map/ppermute | solution.py:318
  22.9 0.0 copy-start.2
  22.9 1.0 copy-done.2
  23.9 0.8 shard_map.61
  24.7 7.3 %collective-permute-start.1 = (bf16[4,24,1024]{2,1,0:T(8,128)(2,1)}, bf16[4,24,1024]{2,1,0:T(8,128)(2,1)}, u32[]{:S(2)}, u32[]{:S(2)}) collective-permute-start(bf16[4,24,1024]{2,1,0:T(8,128)(2,1)} %get-tuple-element.22), channel_id=1, source_target_pairs={{0,64},{64,0},{1,65},{65,1},{2,66},{66,2},{3,67},{67,3},{4,68},{68... | collective-permute-start | bytes 589832 | tf_op jit(solution)/shard_map/ppermute | solution.py:321
  32.0 4.1 %all-to-all-done.plane_ref = bf16[64,16,128]{2,1,0:T(8,128)(2,1)S(1)} async-done(((bf16[64,16,128]{2,1,0:T(8,128)(2,1)}), bf16[64,16,128]{2,1,0:T(8,128)(2,1)S(1)}, u32[]{:S(2)}, u32[]{:S(2)}) %all-to-all-start) | async-done | bytes 262176 | tf_op jit(solution)/shard_map/all_to_all | solution.py:315
  36.1 0.3 shard_map.60
  36.4 0.0 collective-permute-done
  36.4 14.1 %all-gather = bf16[192,2304]{1,0:T(8,128)(2,1)S(1)} all-gather(bf16[48,2304]{1,0:T(8,128)(2,1)S(1)} %shard_map.60), channel_id=2, replica_groups=mesh['x'=4,'yh'=2,'c'=2,'yl'=4,'z'=8] {'x'}, dimensions={0}, use_global_device_ids=true | all-gather | bytes 1105920 | tf_op jit(solution)/shard_map/all_gather | solution.py:324
  50.5 0.0 collective-permute-done.1
  50.5 0.0 collective-permute-done.2.far_ref
  50.5 0.0 copy-done
  50.5 0.0 copy-start.3
  50.5 0.6 copy-done.3
  51.2 4.2 %shard_map.62 = (f32[192,1024]{1,0:T(8,128)}, f32[64,2,128]{2,1,0:T(2,128)}) custom-call(bf16[4,48,2304]{2,1,0:T(8,128)(2,1)S(1)} %bitcast.10, bf16[2304,512]{1,0:T(8,128)(2,1)S(1)} %bitcast.9, bf16[2304,512]{1,0:T(8,128)(2,1)} %collective-permute-done.2.far_ref, f32[24,128]{1,0:T(8,128)S(1)} %get-tuple-element.25.mass_ref, s32[1,24]{1,0:T(1,128)S(1)} %bitcast.11, ...), custom_call_target="tpu_custom_call" | custom-call | tf_op jit(solution)/shard_map/pallas_call | solution.py:77
  55.4 0.0 copy-start.1
  55.4 5.2 %all-to-all-start.1 = ((f32[64,2,128]{2,1,0:T(2,128)}), f32[64,2,128]{2,1,0:T(2,128)S(1)}, u32[]{:S(2)}, u32[]{:S(2)}) async-start(f32[64,2,128]{2,1,0:T(2,128)} %get-tuple-element.27), calls=%async_computation.1 | async-start | bytes 131072 | tf_op jit(solution)/shard_map/all_to_all | solution.py:332
  60.6 1.0 broadcast_select_fusion.1
  61.6 11.2 %all-to-all-done.1.stats_ref = f32[64,2,128]{2,1,0:T(2,128)S(1)} async-done(((f32[64,2,128]{2,1,0:T(2,128)}), f32[64,2,128]{2,1,0:T(2,128)S(1)}, u32[]{:S(2)}, u32[]{:S(2)}) %all-to-all-start.1) | async-done | bytes 65568 | tf_op jit(solution)/shard_map/all_to_all | solution.py:332
  72.8 0.1 shard_map.63
  72.9 10.6 %all_to_all.25.got_ref = bf16[4,48,1152]{2,1,0:T(8,128)(2,1)S(1)} all-to-all(bf16[4,48,1152]{2,1,0:T(8,128)(2,1)S(1)} %shard_map.63), channel_id=1, replica_groups=mesh['x'=4,'yh'=2,'c'=2,'yl'=4,'z'=8] {'x'}, dimensions={0} | all-to-all | bytes 884736 | tf_op jit(solution)/shard_map/all_to_all | solution.py:333
  83.4 0.0 copy-done.1
  83.4 4.5 %shard_map.64 = (bf16[4,48,2304]{2,1,0:T(8,128)(2,1)}, bf16[192,512]{1,0:T(8,128)(2,1)}, bf16[192,512]{1,0:T(8,128)(2,1)}) custom-call(bf16[4,48,1152]{2,1,0:T(8,128)(2,1)S(1)} %all_to_all.25.got_ref, f32[192,1024]{1,0:T(8,128)S(1)} %copy-done.1, bf16[2304,512]{1,0:T(8,128)(2,1)} %bitcast.8, bf16[2304,512]{1,0:T(8,128)(2,1)} %collective-permute-done.2.far_ref), custom_call_target="tpu_custom_call" | custom-call | tf_op jit(solution)/shard_map/pallas_call | solution.py:207
  87.9 0.0 copy-start.5
  87.9 0.0 copy-start.4
  87.9 5.1 %all-to-all-start.3 = ((bf16[4,48,2304]{2,1,0:T(8,128)(2,1)}), bf16[4,48,2304]{2,1,0:T(8,128)(2,1)S(1)}, u32[]{:S(2)}, u32[]{:S(2)}) async-start(bf16[4,48,2304]{2,1,0:T(8,128)(2,1)} %get-tuple-element.31), calls=%async_computation.3 | async-start | bytes 1769472 | tf_op jit(solution)/shard_map/all_to_all | solution.py:344
  93.0 1.9 %collective-permute-start.3 = (bf16[192,2304]{1,0:T(8,128)(2,1)S(1)}, bf16[192,2304]{1,0:T(8,128)(2,1)S(1)}, u32[]{:S(2)}, u32[]{:S(2)}) collective-permute-start(bf16[192,2304]{1,0:T(8,128)(2,1)S(1)} %all-gather), channel_id=1, source_target_pairs={{0,32},{32,0},{1,33},{33,1},{2,34},{34,2},{3,35},{35,3},{4,36},{36... | collective-permute-start | bytes 2654216 | tf_op jit(solution)/shard_map/ppermute | solution.py:337
  94.9 6.6 %all-to-all-done.3.parts_ref = bf16[4,48,2304]{2,1,0:T(8,128)(2,1)S(1)} async-done(((bf16[4,48,2304]{2,1,0:T(8,128)(2,1)}), bf16[4,48,2304]{2,1,0:T(8,128)(2,1)S(1)}, u32[]{:S(2)}, u32[]{:S(2)}) %all-to-all-start.3) | async-done | bytes 884768 | tf_op jit(solution)/shard_map/all_to_all | solution.py:344
  101.6 1.1 shard_map.65
  102.7 4.6 %all-to-all-start.4 = ((bf16[64,16,128]{2,1,0:T(8,128)(2,1)}), bf16[64,16,128]{2,1,0:T(8,128)(2,1)S(1)}, u32[]{:S(2)}, u32[]{:S(2)}) async-start(bf16[64,16,128]{2,1,0:T(8,128)(2,1)} %shard_map.65), calls=%async_computation.4 | async-start | bytes 524288 | tf_op jit(solution)/shard_map/all_to_all | solution.py:345
  107.3 0.0 copy-done.5
  107.3 1.9 %collective-permute-start.4 = (bf16[192,512]{1,0:T(8,128)(2,1)S(1)}, bf16[192,512]{1,0:T(8,128)(2,1)S(1)}, u32[]{:S(2)}, u32[]{:S(2)}) collective-permute-start(bf16[192,512]{1,0:T(8,128)(2,1)S(1)} %copy-done.5), channel_id=1, source_target_pairs={{0,32},{32,0},{1,33},{33,1},{2,34},{34,2},{3,35},{35,3},{4,36},{36... | collective-permute-start | bytes 589832 | tf_op jit(solution)/shard_map/ppermute | solution.py:338
  109.2 0.0 collective-permute-done.3
  109.3 1.4 %collective-permute-done.4 = bf16[192,512]{1,0:T(8,128)(2,1)S(1)} collective-permute-done((bf16[192,512]{1,0:T(8,128)(2,1)S(1)}, bf16[192,512]{1,0:T(8,128)(2,1)S(1)}, u32[]{:S(2)}, u32[]{:S(2)}) %collective-permute-start.4) | collective-permute-done | bytes 196640 | tf_op jit(solution)/shard_map/ppermute | solution.py:338
  110.7 0.0 copy-done.4
  110.7 2.8 %fusion = bf16[2304,1,1,512]{3,0,2,1:T(8,128)(2,1)} fusion(bf16[192,2304]{1,0:T(8,128)(2,1)S(1)} %collective-permute-done.3, bf16[192,2304]{1,0:T(8,128)(2,1)S(1)} %all-gather, bf16[192,512]{1,0:T(8,128)(2,1)S(1)} %collective-permute-done.4, bf16[192,512]{1,0:T(8,128)(2,1)S(1)} %copy-done.4), kind=kOutput, calls=%fused_computation.1 | convolution fusion | flops 911474688 | bytes 4521984 | tf_op jit(solution)/shard_map/dot_general | solution.py:339
  113.5 7.5 %all-to-all-done.4.parts_ref = bf16[64,16,128]{2,1,0:T(8,128)(2,1)S(1)} async-done(((bf16[64,16,128]{2,1,0:T(8,128)(2,1)}), bf16[64,16,128]{2,1,0:T(8,128)(2,1)S(1)}, u32[]{:S(2)}, u32[]{:S(2)}) %all-to-all-start.4) | async-done | bytes 262176 | tf_op jit(solution)/shard_map/all_to_all | solution.py:345
  121.0 0.7 shard_map.66
  (1 shorter events, 0.0 us)
Async XLA Ops:
  0.6 49.9 %copy-start = (bf16[2304,1,1,512]{3,0,2,1:T(8,128)(2,1)S(1)}, bf16[2304,1,1,512]{3,0,2,1:T(8,128)(2,1)}, u32[]{:S(2)}) copy-start(bf16[2304,1,1,512]{3,0,2,1:T(8,128)(2,1)} %param.7) | copy-start | bytes 7077892
  2.3 48.2 %collective-permute-start.2 = (bf16[2304,512]{1,0:T(8,128)(2,1)}, bf16[2304,512]{1,0:T(8,128)(2,1)}, u32[]{:S(2)}, u32[]{:S(2)}) collective-permute-start(bf16[2304,512]{1,0:T(8,128)(2,1)} %bitcast.7), channel_id=1, source_target_pairs={{0,32},{32,0},{1,33},{33,1},{2,34},{34,2},{3,35},{35,3},{4,36},{36... | collective-permute-start | bytes 7077896 | tf_op jit(solution)/shard_map/ppermute | solution.py:317
  4.2 31.9 %all-to-all-start = ((bf16[64,16,128]{2,1,0:T(8,128)(2,1)}), bf16[64,16,128]{2,1,0:T(8,128)(2,1)S(1)}, u32[]{:S(2)}, u32[]{:S(2)}) async-start(bf16[64,16,128]{2,1,0:T(8,128)(2,1)} %shard_map.59), calls=%async_computation | async-start | bytes 524288 | tf_op jit(solution)/shard_map/all_to_all | solution.py:315
  20.8 15.6 %collective-permute-start = (s32[24]{0:T(128)}, s32[24]{0:T(128)S(1)}, u32[]{:S(2)}, u32[]{:S(2)}) collective-permute-start(s32[24]{0:T(128)} %param.5), channel_id=1, source_target_pairs={{0,32},{32,0},{1,33},{33,1},{2,34},{34,2},{3,35},{35,3},{4,36},{36... | collective-permute-start | bytes 296 | tf_op jit(solution)/shard_map/ppermute | solution.py:318
  22.9 1.0 copy-start.2
  24.7 25.8 %collective-permute-start.1 = (bf16[4,24,1024]{2,1,0:T(8,128)(2,1)}, bf16[4,24,1024]{2,1,0:T(8,128)(2,1)}, u32[]{:S(2)}, u32[]{:S(2)}) collective-permute-start(bf16[4,24,1024]{2,1,0:T(8,128)(2,1)} %get-tuple-element.22), channel_id=1, source_target_pairs={{0,64},{64,0},{1,65},{65,1},{2,66},{66,2},{3,67},{67,3},{4,68},{68... | collective-permute-start | bytes 589832 | tf_op jit(solution)/shard_map/ppermute | solution.py:321
  50.5 0.7 copy-start.3
  55.4 28.1 %copy-start.1 = (f32[192,1024]{1,0:T(8,128)S(1)}, f32[192,1024]{1,0:T(8,128)}, u32[]{:S(2)}) copy-start(f32[192,1024]{1,0:T(8,128)} %get-tuple-element.30.tanh_ref) | copy-start | bytes 2359300
  55.4 17.4 %all-to-all-start.1 = ((f32[64,2,128]{2,1,0:T(2,128)}), f32[64,2,128]{2,1,0:T(2,128)S(1)}, u32[]{:S(2)}, u32[]{:S(2)}) async-start(f32[64,2,128]{2,1,0:T(2,128)} %get-tuple-element.27), calls=%async_computation.1 | async-start | bytes 131072 | tf_op jit(solution)/shard_map/all_to_all | solution.py:332
  87.9 19.4 %copy-start.5 = (bf16[192,512]{1,0:T(8,128)(2,1)S(1)}, bf16[192,512]{1,0:T(8,128)(2,1)}, u32[]{:S(2)}) copy-start(bf16[192,512]{1,0:T(8,128)(2,1)} %get-tuple-element.33) | copy-start | bytes 589828
  87.9 22.7 %copy-start.4 = (bf16[192,512]{1,0:T(8,128)(2,1)S(1)}, bf16[192,512]{1,0:T(8,128)(2,1)}, u32[]{:S(2)}) copy-start(bf16[192,512]{1,0:T(8,128)(2,1)} %get-tuple-element.32) | copy-start | bytes 589828
  87.9 13.6 %all-to-all-start.3 = ((bf16[4,48,2304]{2,1,0:T(8,128)(2,1)}), bf16[4,48,2304]{2,1,0:T(8,128)(2,1)S(1)}, u32[]{:S(2)}, u32[]{:S(2)}) async-start(bf16[4,48,2304]{2,1,0:T(8,128)(2,1)} %get-tuple-element.31), calls=%async_computation.3 | async-start | bytes 1769472 | tf_op jit(solution)/shard_map/all_to_all | solution.py:344
  93.0 16.2 %collective-permute-start.3 = (bf16[192,2304]{1,0:T(8,128)(2,1)S(1)}, bf16[192,2304]{1,0:T(8,128)(2,1)S(1)}, u32[]{:S(2)}, u32[]{:S(2)}) collective-permute-start(bf16[192,2304]{1,0:T(8,128)(2,1)S(1)} %all-gather), channel_id=1, source_target_pairs={{0,32},{32,0},{1,33},{33,1},{2,34},{34,2},{3,35},{35,3},{4,36},{36... | collective-permute-start | bytes 2654216 | tf_op jit(solution)/shard_map/ppermute | solution.py:337
  102.7 18.3 %all-to-all-start.4 = ((bf16[64,16,128]{2,1,0:T(8,128)(2,1)}), bf16[64,16,128]{2,1,0:T(8,128)(2,1)S(1)}, u32[]{:S(2)}, u32[]{:S(2)}) async-start(bf16[64,16,128]{2,1,0:T(8,128)(2,1)} %shard_map.65), calls=%async_computation.4 | async-start | bytes 524288 | tf_op jit(solution)/shard_map/all_to_all | solution.py:345
  107.3 3.3 %collective-permute-start.4 = (bf16[192,512]{1,0:T(8,128)(2,1)S(1)}, bf16[192,512]{1,0:T(8,128)(2,1)S(1)}, u32[]{:S(2)}, u32[]{:S(2)}) collective-permute-start(bf16[192,512]{1,0:T(8,128)(2,1)S(1)} %copy-done.5), channel_id=1, source_target_pairs={{0,32},{32,0},{1,33},{33,1},{2,34},{34,2},{3,35},{35,3},{4,36},{36... | collective-permute-start | bytes 589832 | tf_op jit(solution)/shard_map/ppermute | solution.py:338
